TPU v7x, 32 devices: a whole 2x2x4 slice. The times are simulated.
32 devices in a mesh: sect: 4 (over y, x), dom: 8 (over z, core).
Axes of the slice: x: 2, y: 2, z: 4, core: 2. Of those that a mesh axis runs over, the one named last changes fastest.
Arguments:
- fluid_source: float32 [4096, 32, 128], P(('sect', 'dom')), may hold values from -8 to 8
- coef_ids: int32 [4096, 32, 128], P(('sect', 'dom')), may hold values from 0 to 15
- coef_table: float32 [16], replicated, may hold values from 0.5 to 8
- owner_device: int32 [4096, 1], P(('sect', 'dom')), may hold values from 0 to 31; in each aligned block of 128 rows (0 to 127, 128 to 255, ...) at most 8 rows name the same one
- owner_slot: int32 [4096, 1], P(('sect', 'dom')), may hold values from 0 to 127
- solid_init: float32 [4096, 128], P(('sect', 'dom')), may hold values from -4 to 4
- solid_load: float32 [4096, 128], P(('sect', 'dom')), may hold values from -6 to 6
- compliance: float32 [128, 128], replicated, may hold values from -0.5 to 0.5
Outputs:
- fluid_state: float32 [4096, 32, 128], P(('sect', 'dom'))
- displacement: float32 [4096, 128], P(('sect', 'dom'))
- coupling_norms: float32 [2], replicated
Inputs may be any that keep to these rules, and one draw needn't show every extreme that they name: `owner_device`: among the 128 rows of one device no owner device is named more than 8 times, a bound that some block reaches.
All inputs are finite; a program needn't handle non-finite values.
Results may differ from a plain program's by a relative error of at most 0.0001.
Values sent between devices are 32-bit elements; how exact they have to be, the bound alone decides.
A program may use at most 64 MiB of HBM per device.

v0:
```python
import jax
import jax.numpy as jnp
from jax import lax
from jax.sharding import PartitionSpec as P

SWEEPS = 3
COUPLE = 2


relax_factor = 0.5


def with_halo(block, sides, width):
    for axis, dim in sides:
        count = lax.axis_size(axis)
        forward = [(i, i + 1) for i in range(count - 1)]
        backward = [(target, source) for source, target in forward]
        low = lax.ppermute(
            lax.slice_in_dim(block, block.shape[dim] - width, None, axis=dim), axis, forward
        )
        high = lax.ppermute(lax.slice_in_dim(block, 0, width, axis=dim), axis, backward)
        block = jnp.concatenate([low, block, high], axis=dim)
    return block


def neighbours(padded):
    center = padded[1:-1]
    total = padded[2:] + padded[:-2]
    wide_y = jnp.pad(center, ((0, 0), (1, 1), (0, 0)))
    total = total + wide_y[:, 2:, :] + wide_y[:, :-2, :]
    wide_z = jnp.pad(center, ((0, 0), (0, 0), (1, 1)))
    total = total + wide_z[:, :, 2:] + wide_z[:, :, :-2]
    return total


def route_requests(buffer):
    return lax.all_to_all(buffer, ("sect", "dom"), split_axis=0, concat_axis=0, tiled=True)


def route_wall(buffer):
    return lax.all_to_all(buffer, ("sect", "dom"), split_axis=0, concat_axis=0, tiled=True)


def route_traction(buffer):
    return lax.all_to_all(buffer, ("sect", "dom"), split_axis=0, concat_axis=0, tiled=True)


def per_device(
    fluid_source, coef_ids, coef_table, owner_device, owner_slot, solid_init, solid_load, compliance
):
    sect_count = lax.axis_size("sect")
    dom_count = lax.axis_size("dom")
    devices = sect_count * dom_count
    fluid_rows = fluid_source.shape[0]
    row_width = fluid_source.shape[2]
    solid_rows = solid_init.shape[0]
    capacity = 2 * fluid_rows // devices
    highest = lax.Precision.HIGHEST
    diagonal = jnp.full(coef_ids.shape, 6.0, jnp.float32)
    for table_index in range(coef_table.shape[0]):
        diagonal = diagonal + jnp.where(coef_ids == table_index, coef_table[table_index], 0.0)
    destination = owner_device[:, 0]
    owner_hits = (destination[:, None] == jnp.arange(devices, dtype=jnp.int32)[None, :]).astype(
        jnp.int32
    )
    earlier = jnp.cumsum(owner_hits, axis=0) - owner_hits
    ranking = jnp.sum(earlier * owner_hits, axis=1)
    position = destination * capacity + ranking
    slot_places = jnp.arange(devices * capacity, dtype=jnp.int32)
    matches = position[None, :] == slot_places[:, None]
    send_slot = jnp.sum(jnp.where(matches, owner_slot[:, 0][None, :] + 1, 0), axis=1) - 1
    placer = matches.astype(jnp.float32)
    got_slot = route_requests(send_slot.reshape(devices, capacity)).reshape(-1)
    picker = (got_slot[:, None] == jnp.arange(solid_rows, dtype=jnp.int32)[None, :]).astype(
        jnp.float32
    )
    fluid_state = jnp.zeros(fluid_source.shape, jnp.float32)
    displacement = solid_init
    partials = []
    for iteration in range(COUPLE):
        answer = jnp.dot(picker, displacement, precision=highest)
        returned = route_wall(answer.reshape(devices, capacity, row_width)).reshape(-1, row_width)
        wall_rows = lax.dot_general(placer, returned, (((0,), (0,)), ((), ())), precision=highest)
        source = fluid_source.at[:, 0, :].add(wall_rows)
        for sweep_index in range(SWEEPS):
            padded = with_halo(fluid_state, ((("sect", "dom"), 0),), 1)
            fluid_state = (source + neighbours(padded)) / diagonal
        traction = fluid_state[:, 0, :] - fluid_state[:, 1, :]
        outgoing = jnp.dot(placer, traction, precision=highest).reshape(
            devices, capacity, row_width
        )
        incoming = route_traction(outgoing).reshape(-1, row_width)
        solid_force = (
            lax.dot_general(picker, incoming, (((0,), (0,)), ((), ())), precision=highest)
            + solid_load
        )
        trial_disp = jnp.dot(solid_force, compliance, precision=highest)
        mismatch = trial_disp - displacement
        local_sum = jnp.sum(mismatch * mismatch)
        partials.append(local_sum)
        displacement = displacement + relax_factor * mismatch
    totals = lax.psum(jnp.stack(partials), ("sect", "dom"))
    coupling_norms = jnp.sqrt(totals + 1e-06)
    return (fluid_state, displacement, coupling_norms)


def solution(mesh):
    placed = (
        P(("sect", "dom"), None, None),
        P(("sect", "dom"), None, None),
        P(),
        P(("sect", "dom"), None),
        P(("sect", "dom"), None),
        P(("sect", "dom"), None),
        P(("sect", "dom"), None),
        P(),
    )
    return jax.shard_map(
        per_device,
        mesh=mesh,
        in_specs=placed,
        out_specs=(P(("sect", "dom"), None, None), P(("sect", "dom"), None), P()),
        check_vma=False,
    )
```

profile of v0, /device:TPU:0, one launch (start us, length us, event | category | flops | bytes accessed | tf_op | source)
XLA Modules:
  0.0 268.1 jit_solution(16818036980260471210)
XLA Ops:
  0.7 1.6 copy.29
  3.0 14.3 %all_to_all.26 = s32[32,1,8]{2,1,0:T(1,128)S(1)} all-to-all(s32[32,1,8]{2,1,0:T(1,128)S(1)} %bitcast.67), channel_id=1, replica_groups=mesh['sect'=4,'dom'=8] {'sect','dom'}, dimensions={0} | all-to-all | bytes 2048 | tf_op jit(solution)/shard_map/all_to_all | solution.py:37
  19.5 2.6 all-to-all-start.1
  23.3 3.0 %collective-permute-start.1 = (f32[1,32,128]{2,1,0:T(8,128)S(1)}, f32[1,32,128]{2,1,0:T(8,128)S(1)}, u32[]{:S(2)}, u32[]{:S(2)}) collective-permute-start(f32[1,32,128]{2,1,0:T(8,128)S(1)} %broadcast.129), channel_id=1, source_target_pairs={{0,1},{1,2},{2,3},{3,4},{4,5},{5,6},{6,7},{7,8},{8,9},{9,10},{10,1... | collective-permute-start | bytes 49160 | tf_op jit(solution)/shard_map/ppermute | solution.py:18
  28.5 1.7 all-to-all-done.1
  30.5 3.0 %scatter-add.6 = f32[128,32,128]{2,1,0:T(8,128)} dynamic-update-slice(f32[128,32,128]{2,1,0:T(8,128)} %copy-done.2, f32[128,1,128]{2,1,0:T(1,128)S(1)} %bitcast.64, s32[]{:T(128)} %constant.80.clone.1, s32[]{:T(128)} %constant.80.clone.1, s32[]{:T(128)} %constant.80.clone.1) | dynamic-update-slice | bytes 131076 | tf_op jit(solution)/shard_map/scatter-add | solution.py:84
  33.8 16.0 %fusion.6 = f32[128,32,128]{2,1,0:T(8,128)S(1)} fusion(f32[128,32,128]{2,1,0:T(8,128)} %scatter-add.6, f32[1,32,128]{2,1,0:T(8,128)S(1)} %collective-permute-done, f32[1,32,128]{2,1,0:T(8,128)S(1)} %collective-permute-done.1, f32[128,32,128]{2,1,0:T(8,128)S(1)} %broadcast_in_dim.90, f32[]{:T(128)} %bitcast.22, s32[128,32,128]{2,1,0:T(8,128)S(1)} %copy-done.1, ...), kind=kLoop, calls=%fused_computation.32 | loop fusion | flops 28835840 | bytes 8421440 | tf_op jit(solution)/shard_map/div | solution.py:87
  51.0 3.0 %collective-permute-start.3 = (f32[1,32,128]{2,1,0:T(8,128)S(1)}, f32[1,32,128]{2,1,0:T(8,128)S(1)}, u32[]{:S(2)}, u32[]{:S(2)}) collective-permute-start(f32[1,32,128]{2,1,0:T(8,128)S(1)} %get-tuple-element.36), channel_id=1, source_target_pairs={{0,1},{1,2},{2,3},{3,4},{4,5},{5,6},{6,7},{7,8},{8,9},{9,10},{10,1... | collective-permute-start | bytes 49160 | tf_op jit(solution)/shard_map/ppermute | solution.py:18
  54.9 15.2 %fusion.12 = f32[128,32,128]{2,1,0:T(8,128)S(1)} fusion(f32[128,32,128]{2,1,0:T(8,128)S(1)} %copy-done.3, f32[128,32,128]{2,1,0:T(8,128)S(1)} %fusion.6, f32[1,32,128]{2,1,0:T(8,128)S(1)} %collective-permute-done.3, f32[1,32,128]{2,1,0:T(8,128)S(1)} %collective-permute-done.2, f32[]{:T(128)} %bitcast.22, s32[128,32,128]{2,1,0:T(8,128)S(1)} %copy-done.1, ...), kind=kLoop, calls=%fused_computation.38 | loop fusion | flops 29884416 | bytes 8421440 | tf_op jit(solution)/shard_map/div | solution.py:87
  71.4 4.1 %collective-permute-start.5 = (f32[1,32,128]{2,1,0:T(8,128)S(1)}, f32[1,32,128]{2,1,0:T(8,128)S(1)}, u32[]{:S(2)}, u32[]{:S(2)}) collective-permute-start(f32[1,32,128]{2,1,0:T(8,128)S(1)} %get-tuple-element.34), channel_id=1, source_target_pairs={{0,1},{1,2},{2,3},{3,4},{4,5},{5,6},{6,7},{7,8},{8,9},{9,10},{10,1... | collective-permute-start | bytes 49160 | tf_op jit(solution)/shard_map/ppermute | solution.py:18
  76.4 15.2 %fusion.18 = f32[128,32,128]{2,1,0:T(8,128)S(1)} fusion(f32[128,32,128]{2,1,0:T(8,128)S(1)} %copy-done.3, f32[128,32,128]{2,1,0:T(8,128)S(1)} %fusion.12, f32[1,32,128]{2,1,0:T(8,128)S(1)} %collective-permute-done.5, f32[1,32,128]{2,1,0:T(8,128)S(1)} %collective-permute-done.4, f32[]{:T(128)} %bitcast.22, s32[128,32,128]{2,1,0:T(8,128)S(1)} %copy-done.1, ...), kind=kLoop, calls=%fused_computation.44 | loop fusion | flops 29884416 | bytes 8421440 | tf_op jit(solution)/shard_map/div | solution.py:87
  93.3 27.0 %all_to_all.27 = f32[32,8,128]{2,1,0:T(8,128)S(1)} all-to-all(f32[32,8,128]{2,1,0:T(8,128)S(1)} %fusion.46), channel_id=1, replica_groups=mesh['sect'=4,'dom'=8] {'sect','dom'}, dimensions={0} | all-to-all | bytes 262144 | tf_op jit(solution)/shard_map/all_to_all | solution.py:45
  121.8 2.6 all-to-all-start.3
  126.4 3.0 %collective-permute-start.7 = (f32[1,32,128]{2,1,0:T(8,128)S(1)}, f32[1,32,128]{2,1,0:T(8,128)S(1)}, u32[]{:S(2)}, u32[]{:S(2)}) collective-permute-start(f32[1,32,128]{2,1,0:T(8,128)S(1)} %get-tuple-element.32), channel_id=1, source_target_pairs={{0,1},{1,2},{2,3},{3,4},{4,5},{5,6},{6,7},{7,8},{8,9},{9,10},{10,1... | collective-permute-start | bytes 49160 | tf_op jit(solution)/shard_map/ppermute | solution.py:18
  129.4 3.1 %all-to-all-done.3 = f32[32,8,128]{2,1,0:T(8,128)S(1)} async-done(((f32[32,8,128]{2,1,0:T(8,128)}), f32[32,8,128]{2,1,0:T(8,128)S(1)}, u32[]{:S(2)}, u32[]{:S(2)}) %all-to-all-start.3) | async-done | bytes 131104 | tf_op jit(solution)/shard_map/all_to_all | solution.py:41
  132.8 2.9 %scatter-add.9 = f32[128,32,128]{2,1,0:T(8,128)} dynamic-update-slice(f32[128,32,128]{2,1,0:T(8,128)} %copy.27, f32[128,1,128]{2,1,0:T(1,128)S(1)} %bitcast.63, s32[]{:T(128)} %constant.80.clone.1, s32[]{:T(128)} %constant.80.clone.1, s32[]{:T(128)} %constant.80.clone.1) | dynamic-update-slice | bytes 131076 | tf_op jit(solution)/shard_map/scatter-add | solution.py:84
  135.8 21.2 %fusion.24 = f32[128,32,128]{2,1,0:T(8,128)S(1)} fusion(f32[128,32,128]{2,1,0:T(8,128)} %scatter-add.9, f32[128,32,128]{2,1,0:T(8,128)} %copy-done.5, f32[1,32,128]{2,1,0:T(8,128)S(1)} %collective-permute-done.7, f32[1,32,128]{2,1,0:T(8,128)S(1)} %collective-permute-done.6, f32[]{:T(128)} %bitcast.22, s32[128,32,128]{2,1,0:T(8,128)S(1)} %copy-done.1, ...), kind=kLoop, calls=%fused_computation.50 | loop fusion | flops 29884416 | bytes 8421440 | tf_op jit(solution)/shard_map/div | solution.py:87
  158.3 3.2 %collective-permute-start.9 = (f32[1,32,128]{2,1,0:T(8,128)S(1)}, f32[1,32,128]{2,1,0:T(8,128)S(1)}, u32[]{:S(2)}, u32[]{:S(2)}) collective-permute-start(f32[1,32,128]{2,1,0:T(8,128)S(1)} %get-tuple-element.30), channel_id=1, source_target_pairs={{0,1},{1,2},{2,3},{3,4},{4,5},{5,6},{6,7},{7,8},{8,9},{9,10},{10,1... | collective-permute-start | bytes 49160 | tf_op jit(solution)/shard_map/ppermute | solution.py:18
  162.2 15.2 %fusion.30 = f32[128,32,128]{2,1,0:T(8,128)S(1)} fusion(f32[128,32,128]{2,1,0:T(8,128)S(1)} %copy-done.4, f32[128,32,128]{2,1,0:T(8,128)S(1)} %fusion.24, f32[1,32,128]{2,1,0:T(8,128)S(1)} %collective-permute-done.9, f32[1,32,128]{2,1,0:T(8,128)S(1)} %collective-permute-done.8, f32[]{:T(128)} %bitcast.22, s32[128,32,128]{2,1,0:T(8,128)S(1)} %copy-done.1, ...), kind=kLoop, calls=%fused_computation.56 | loop fusion | flops 29884416 | bytes 8421440 | tf_op jit(solution)/shard_map/div | solution.py:87
  178.7 4.1 %collective-permute-start.11 = (f32[1,32,128]{2,1,0:T(8,128)S(1)}, f32[1,32,128]{2,1,0:T(8,128)S(1)}, u32[]{:S(2)}, u32[]{:S(2)}) collective-permute-start(f32[1,32,128]{2,1,0:T(8,128)S(1)} %get-tuple-element.28), channel_id=1, source_target_pairs={{0,1},{1,2},{2,3},{3,4},{4,5},{5,6},{6,7},{7,8},{8,9},{9,10},{10,1... | collective-permute-start | bytes 49160 | tf_op jit(solution)/shard_map/ppermute | solution.py:18
  183.7 15.2 %fusion.36 = f32[128,32,128]{2,1,0:T(8,128)S(1)} fusion(f32[128,32,128]{2,1,0:T(8,128)S(1)} %copy-done.4, f32[128,32,128]{2,1,0:T(8,128)S(1)} %fusion.30, f32[1,32,128]{2,1,0:T(8,128)S(1)} %collective-permute-done.11, f32[1,32,128]{2,1,0:T(8,128)S(1)} %collective-permute-done.10, f32[]{:T(128)} %bitcast.22, s32[128,32,128]{2,1,0:T(8,128)S(1)} %copy-done.1, ...), kind=kLoop, calls=%fused_computation.62 | loop fusion | flops 29884416 | bytes 8421440 | tf_op jit(solution)/shard_map/div | solution.py:87
  200.5 25.6 %all_to_all.28 = f32[32,8,128]{2,1,0:T(8,128)S(1)} all-to-all(f32[32,8,128]{2,1,0:T(8,128)S(1)} %fusion.44), channel_id=1, replica_groups=mesh['sect'=4,'dom'=8] {'sect','dom'}, dimensions={0} | all-to-all | bytes 262144 | tf_op jit(solution)/shard_map/all_to_all | solution.py:45
  226.5 1.5 multiply_reduce_fusion.1
  229.3 38.3 %psum.7 = f32[2]{0:T(128)S(1)} all-reduce(f32[2]{0:T(128)S(1)} %pad_maximum_fusion.10), channel_id=1, replica_groups=mesh['sect'=4,'dom'=8] {'sect','dom'}, use_global_device_ids=true, to_apply=%region_5.6 | all-reduce | flops 2 | bytes 16 | tf_op jit(solution)/shard_map/psum | solution.py:102
  (77 shorter events, 24.4 us)
Async XLA Ops:
  0.6 120.0 %copy-start = (f32[128,128]{1,0:T(8,128)S(1)}, f32[128,128]{1,0:T(8,128)}, u32[]{:S(2)}) copy-start(f32[128,128]{1,0:T(8,128)} %param.19) | copy-start | bytes 196612
  0.6 1.7 copy-start.10
  0.7 2.1 copy-start.11
  0.7 17.9 %copy-start.7 = (f32[128,128]{1,0:T(8,128)S(1)}, f32[128,128]{1,0:T(8,128)}, u32[]{:S(2)}) copy-start(f32[128,128]{1,0:T(8,128)} %param.17) | copy-start | bytes 196612
  2.3 24.1 %copy-start.2 = (f32[128,32,128]{2,1,0:T(8,128)}, f32[128,32,128]{2,1,0:T(8,128)S(1)}, u32[]{:S(2)}) copy-start(f32[128,32,128]{2,1,0:T(8,128)S(1)} %copy.29) | copy-start | bytes 6291460
  19.5 10.7 %all-to-all-start.1 = ((f32[32,8,128]{2,1,0:T(8,128)}), f32[32,8,128]{2,1,0:T(8,128)S(1)}, u32[]{:S(2)}, u32[]{:S(2)}) async-start(f32[32,8,128]{2,1,0:T(8,128)} %convolution_bitcast_fusion.1), calls=%async_computation.1 | async-start | bytes 262144 | tf_op jit(solution)/shard_map/all_to_all | solution.py:41
  22.0 11.4 %collective-permute-start = (f32[1,32,128]{2,1,0:T(8,128)S(1)}, f32[1,32,128]{2,1,0:T(8,128)S(1)}, u32[]{:S(2)}, u32[]{:S(2)}) collective-permute-start(f32[1,32,128]{2,1,0:T(8,128)S(1)} %broadcast.129), channel_id=1, source_target_pairs={{1,0},{2,1},{3,2},{4,3},{5,4},{6,5},{7,6},{8,7},{9,8},{10,9},{11,1... | collective-permute-start | bytes 49160 | tf_op jit(solution)/shard_map/ppermute | solution.py:21
  23.3 10.1 %collective-permute-start.1 = (f32[1,32,128]{2,1,0:T(8,128)S(1)}, f32[1,32,128]{2,1,0:T(8,128)S(1)}, u32[]{:S(2)}, u32[]{:S(2)}) collective-permute-start(f32[1,32,128]{2,1,0:T(8,128)S(1)} %broadcast.129), channel_id=1, source_target_pairs={{0,1},{1,2},{2,3},{3,4},{4,5},{5,6},{6,7},{7,8},{8,9},{9,10},{10,1... | collective-permute-start | bytes 49160 | tf_op jit(solution)/shard_map/ppermute | solution.py:18
  27.8 5.9 %copy-start.1 = (s32[128,32,128]{2,1,0:T(8,128)S(1)}, s32[128,32,128]{2,1,0:T(8,128)}, u32[]{:S(2)}) copy-start(s32[128,32,128]{2,1,0:T(8,128)} %param.13) | copy-start | bytes 6291460
  33.7 21.2 %copy-start.3 = (f32[128,32,128]{2,1,0:T(8,128)S(1)}, f32[128,32,128]{2,1,0:T(8,128)}, u32[]{:S(2)}) copy-start(f32[128,32,128]{2,1,0:T(8,128)} %scatter-add.6) | copy-start | bytes 6291460
  49.7 4.3 %collective-permute-start.2 = (f32[1,32,128]{2,1,0:T(8,128)S(1)}, f32[1,32,128]{2,1,0:T(8,128)S(1)}, u32[]{:S(2)}, u32[]{:S(2)}) collective-permute-start(f32[1,32,128]{2,1,0:T(8,128)S(1)} %get-tuple-element.35), channel_id=1, source_target_pairs={{1,0},{2,1},{3,2},{4,3},{5,4},{6,5},{7,6},{8,7},{9,8},{10,9},{11,1... | collective-permute-start | bytes 49160 | tf_op jit(solution)/shard_map/ppermute | solution.py:21
  51.0 3.9 %collective-permute-start.3 = (f32[1,32,128]{2,1,0:T(8,128)S(1)}, f32[1,32,128]{2,1,0:T(8,128)S(1)}, u32[]{:S(2)}, u32[]{:S(2)}) collective-permute-start(f32[1,32,128]{2,1,0:T(8,128)S(1)} %get-tuple-element.36), channel_id=1, source_target_pairs={{0,1},{1,2},{2,3},{3,4},{4,5},{5,6},{6,7},{7,8},{8,9},{9,10},{10,1... | collective-permute-start | bytes 49160 | tf_op jit(solution)/shard_map/ppermute | solution.py:18
  70.1 5.5 %collective-permute-start.4 = (f32[1,32,128]{2,1,0:T(8,128)S(1)}, f32[1,32,128]{2,1,0:T(8,128)S(1)}, u32[]{:S(2)}, u32[]{:S(2)}) collective-permute-start(f32[1,32,128]{2,1,0:T(8,128)S(1)} %get-tuple-element.33), channel_id=1, source_target_pairs={{1,0},{2,1},{3,2},{4,3},{5,4},{6,5},{7,6},{8,7},{9,8},{10,9},{11,1... | collective-permute-start | bytes 49160 | tf_op jit(solution)/shard_map/ppermute | solution.py:21
  71.4 5.0 %collective-permute-start.5 = (f32[1,32,128]{2,1,0:T(8,128)S(1)}, f32[1,32,128]{2,1,0:T(8,128)S(1)}, u32[]{:S(2)}, u32[]{:S(2)}) collective-permute-start(f32[1,32,128]{2,1,0:T(8,128)S(1)} %get-tuple-element.34), channel_id=1, source_target_pairs={{0,1},{1,2},{2,3},{3,4},{4,5},{5,6},{6,7},{7,8},{8,9},{9,10},{10,1... | collective-permute-start | bytes 49160 | tf_op jit(solution)/shard_map/ppermute | solution.py:18
  75.6 44.7 %copy-start.8 = (f32[128,128]{1,0:T(8,128)S(1)}, f32[128,128]{1,0:T(8,128)}, u32[]{:S(2)}) copy-start(f32[128,128]{1,0:T(8,128)} %param.18) | copy-start | bytes 196612
  91.6 1.3 copy-start.5
  121.8 10.7 %all-to-all-start.3 = ((f32[32,8,128]{2,1,0:T(8,128)}), f32[32,8,128]{2,1,0:T(8,128)S(1)}, u32[]{:S(2)}, u32[]{:S(2)}) async-start(f32[32,8,128]{2,1,0:T(8,128)} %convolution_bitcast_fusion), calls=%async_computation.3 | async-start | bytes 262144 | tf_op jit(solution)/shard_map/all_to_all | solution.py:41
  125.1 10.7 %collective-permute-start.6 = (f32[1,32,128]{2,1,0:T(8,128)S(1)}, f32[1,32,128]{2,1,0:T(8,128)S(1)}, u32[]{:S(2)}, u32[]{:S(2)}) collective-permute-start(f32[1,32,128]{2,1,0:T(8,128)S(1)} %get-tuple-element.31), channel_id=1, source_target_pairs={{1,0},{2,1},{3,2},{4,3},{5,4},{6,5},{7,6},{8,7},{9,8},{10,9},{11,1... | collective-permute-start | bytes 49160 | tf_op jit(solution)/shard_map/ppermute | solution.py:21
  126.4 9.4 %collective-permute-start.7 = (f32[1,32,128]{2,1,0:T(8,128)S(1)}, f32[1,32,128]{2,1,0:T(8,128)S(1)}, u32[]{:S(2)}, u32[]{:S(2)}) collective-permute-start(f32[1,32,128]{2,1,0:T(8,128)S(1)} %get-tuple-element.32), channel_id=1, source_target_pairs={{0,1},{1,2},{2,3},{3,4},{4,5},{5,6},{6,7},{7,8},{8,9},{9,10},{10,1... | collective-permute-start | bytes 49160 | tf_op jit(solution)/shard_map/ppermute | solution.py:18
  135.7 26.4 %copy-start.4 = (f32[128,32,128]{2,1,0:T(8,128)S(1)}, f32[128,32,128]{2,1,0:T(8,128)}, u32[]{:S(2)}) copy-start(f32[128,32,128]{2,1,0:T(8,128)} %scatter-add.9) | copy-start | bytes 6291460
  157.0 4.5 %collective-permute-start.8 = (f32[1,32,128]{2,1,0:T(8,128)S(1)}, f32[1,32,128]{2,1,0:T(8,128)S(1)}, u32[]{:S(2)}, u32[]{:S(2)}) collective-permute-start(f32[1,32,128]{2,1,0:T(8,128)S(1)} %get-tuple-element.29), channel_id=1, source_target_pairs={{1,0},{2,1},{3,2},{4,3},{5,4},{6,5},{7,6},{8,7},{9,8},{10,9},{11,1... | collective-permute-start | bytes 49160 | tf_op jit(solution)/shard_map/ppermute | solution.py:21
  158.3 3.9 %collective-permute-start.9 = (f32[1,32,128]{2,1,0:T(8,128)S(1)}, f32[1,32,128]{2,1,0:T(8,128)S(1)}, u32[]{:S(2)}, u32[]{:S(2)}) collective-permute-start(f32[1,32,128]{2,1,0:T(8,128)S(1)} %get-tuple-element.30), channel_id=1, source_target_pairs={{0,1},{1,2},{2,3},{3,4},{4,5},{5,6},{6,7},{7,8},{8,9},{9,10},{10,1... | collective-permute-start | bytes 49160 | tf_op jit(solution)/shard_map/ppermute | solution.py:18
  177.4 5.4 %collective-permute-start.10 = (f32[1,32,128]{2,1,0:T(8,128)S(1)}, f32[1,32,128]{2,1,0:T(8,128)S(1)}, u32[]{:S(2)}, u32[]{:S(2)}) collective-permute-start(f32[1,32,128]{2,1,0:T(8,128)S(1)} %get-tuple-element.27), channel_id=1, source_target_pairs={{1,0},{2,1},{3,2},{4,3},{5,4},{6,5},{7,6},{8,7},{9,8},{10,9},{11,1... | collective-permute-start | bytes 49160 | tf_op jit(solution)/shard_map/ppermute | solution.py:21
  178.7 4.9 %collective-permute-start.11 = (f32[1,32,128]{2,1,0:T(8,128)S(1)}, f32[1,32,128]{2,1,0:T(8,128)S(1)}, u32[]{:S(2)}, u32[]{:S(2)}) collective-permute-start(f32[1,32,128]{2,1,0:T(8,128)S(1)} %get-tuple-element.28), channel_id=1, source_target_pairs={{0,1},{1,2},{2,3},{3,4},{4,5},{5,6},{6,7},{7,8},{8,9},{9,10},{10,1... | collective-permute-start | bytes 49160 | tf_op jit(solution)/shard_map/ppermute | solution.py:18
  (2 other events, 2.7 us)
where the time goes:
time: 270 us; the launch traced here: 268 us
  blocking collectives  105 us (39%)
  other arithmetic  101 us (37%)
  starting transfers between devices  33.4 us (12%)
  local copies, waits for them, and re-layouts  14 us (5%)
  waiting for transfers between devices  7.84 us (3%)
  matrix products  5.28 us (2%)
    div x6, other arithmetic, per_device(): fluid_state = (source + neighbours(padded)) / diagonal  98.1 us
    all_to_all x2, blocking collectives, route_traction(): lax.all_to_all(buffer, ('sect', 'dom'), split_axis=0, concat_axis=0, tile...  52.6 us
    psum x1, blocking collectives, per_device(): totals = lax.psum(jnp.stack(partials), ('sect', 'dom'))  38.3 us
    ppermute x6, starting transfers between devices, with_halo(): lax.ppermute(lax.slice_in_dim(block, block.shape[dim] - width, None, axis...  20.6 us
    all_to_all x1, blocking collectives, route_requests(): lax.all_to_all(buffer, ('sect', 'dom'), split_axis=0, concat_axis=0, tile...  14.3 us
    ppermute x6, starting transfers between devices, with_halo(): lax.ppermute(lax.slice_in_dim(block, 0, width, axis=dim), axis, backward)  7.74 us
    scatter-add x2, local copies, waits for them, and re-layouts, per_device(): source = fluid_source.at[:, 0, :].add(wall_rows)  5.9 us
    unnamed x26, local copies, waits for them, and re-layouts  5.67 us
  transfers between devices with their start and end apart: 14, of which 6 were waited for; matrix products, arithmetic and copies ran while one was open for 3% of the time, Pallas kernels for 0%

commit v1 on v0

v1 whole, which is shorter than its diff:
```python
import functools

import jax
import jax.numpy as jnp
from jax import lax
from jax.experimental import pallas as pl
from jax.experimental.pallas import tpu as pltpu
from jax.sharding import PartitionSpec as P

SWEEPS = 3
COUPLE = 2
RELAX = 0.5
TOTAL = SWEEPS * COUPLE
GHOST = TOTAL - 1
PAD = 8
MESH = pl.DeviceIdType.MESH


def iota(shape, dim):
    return lax.broadcasted_iota(jnp.int32, shape, dim)


def pieces(x):
    high = x.astype(jnp.bfloat16)
    low = (x - high.astype(jnp.float32)).astype(jnp.bfloat16)
    return high, low


def pick(onehot, x):
    width = x.shape[1]
    both = jnp.concatenate(pieces(x), axis=1)
    out = jnp.dot(onehot, both, preferred_element_type=jnp.float32)
    return out[:, :width] + out[:, width:]


def product(x, y):
    xh, xl = pieces(x)
    yh, yl = pieces(y)
    left = jnp.concatenate([xh, xh, xl], axis=1)
    right = jnp.concatenate([yh, yl, yh], axis=0)
    return jnp.dot(left, right, preferred_element_type=jnp.float32)


def beside(x):
    rows, width = x.shape
    lane = iota(x.shape, 1)
    low = jnp.where(lane == 0, 0.0, pltpu.roll(x, 1, 1))
    high = jnp.where(lane == width - 1, 0.0, pltpu.roll(x, width - 1, 1))
    return low + high


def kernel(
    n, dom, source, ids, table, owner, slot, init, load, compliance,
    state_out, disp_out, norm_out,
    src, idv, inv, even, odd, invp, base, walls, force,
    place, place_t, choose, choose_t,
    req_s, req_r, wall_s, wall_r, trac_s, trac_r, norm_s, norm_r,
    in_sem, out_sem, ghost_ss, ghost_rs, a2a_ss, a2a_rs, edge_ss, edge_rs,
):
    rows, depth, width = source.shape
    end = PAD + rows
    cap = PAD
    me = lax.axis_index("sect") * dom + lax.axis_index("dom")

    def coords(index):
        return (lax.div(index, dom), lax.rem(index, dom))

    right = coords(lax.rem(me + 1, n))
    left = coords(lax.rem(me + n - 1, n))

    loads = [
        pltpu.make_async_copy(source, src.at[pl.ds(PAD, rows)], in_sem.at[0]),
        pltpu.make_async_copy(ids, idv.at[pl.ds(PAD, rows)], in_sem.at[1]),
    ]
    for copy in loads:
        copy.start()

    barrier = pltpu.get_barrier_semaphore()

    def greet(k, carry):
        pl.semaphore_signal(
            barrier, inc=1, device_id=coords(lax.rem(me + k, n)), device_id_type=MESH
        )
        return carry

    lax.fori_loop(1, n, greet, 0)

    owner_row = owner[...]
    slot_row = slot[...]
    hits = (iota((n, rows), 0) == owner_row).astype(jnp.float32)
    before = (iota((rows, rows), 0) < iota((rows, rows), 1)).astype(jnp.bfloat16)
    earlier = jnp.dot(hits.astype(jnp.bfloat16), before, preferred_element_type=jnp.float32)
    rank = jnp.sum(earlier * hits, axis=0, keepdims=True).astype(jnp.int32)
    position = owner_row * cap + rank
    placed = (iota((n * cap, rows), 0) == position).astype(jnp.float32)
    place[...] = placed.astype(jnp.bfloat16)
    place_t[...] = placed.T.astype(jnp.bfloat16)
    wanted = jnp.sum(placed * (slot_row + 1).astype(jnp.float32), axis=1, keepdims=True) - 1.0
    wanted = wanted.reshape(n, cap, 1)
    square = iota((n, cap, width), 2) == iota((n, cap, width), 1)
    req_s[...] = jnp.sum(jnp.where(square, wanted, 0.0), axis=1, keepdims=True).astype(jnp.int32)

    pl.semaphore_wait(barrier, n - 1)

    def exchange(sent, got, phase):
        def one(k, carry):
            peer = lax.rem(me + k, n)
            pltpu.make_async_remote_copy(
                src_ref=sent.at[peer],
                dst_ref=got.at[me],
                send_sem=a2a_ss.at[phase],
                recv_sem=a2a_rs.at[phase],
                device_id=coords(peer),
                device_id_type=MESH,
            ).start()
            return carry

        lax.fori_loop(1, n, one, 0)
        got[me] = sent[me]

    def finish(ref, sem):
        part = ref.at[pl.ds(0, n - 1)]
        pltpu.make_async_copy(part, part, sem).wait()

    exchange(req_s, req_r, 0)

    def to_neighbours(from_low, from_high, to_low, to_high, ss, rs):
        copies = [
            pltpu.make_async_remote_copy(
                src_ref=a, dst_ref=b, send_sem=ss(i), recv_sem=rs(i),
                device_id=device, device_id_type=MESH,
            )
            for i, (a, b, device) in enumerate(
                ((from_low, to_high, left), (from_high, to_low, right))
            )
        ]
        for copy in copies:
            copy.start()
        return copies

    ghosts = []
    for number, (whole, held) in enumerate(((source, src), (ids, idv))):
        ghosts += to_neighbours(
            whole.at[pl.ds(0, GHOST)], whole.at[pl.ds(rows - GHOST, GHOST)],
            held.at[pl.ds(PAD - GHOST, GHOST)], held.at[pl.ds(end, GHOST)],
            lambda i: ghost_ss.at[number, i], lambda i: ghost_rs.at[number, i],
        )

    lane = iota((depth, width), 1)
    recip = jnp.zeros((depth, width), jnp.float32)
    for entry in range(table.shape[0]):
        recip = jnp.where(lane == entry, table[entry], recip)
    recip = 1.0 / (6.0 + recip)

    def first(x, scale):
        value = jnp.take_along_axis(recip, idv[x], axis=1, mode="promise_in_bounds")
        if scale is not None:
            value = value * scale
        inv[x] = value
        even[x] = src[x] * value

    for copy in loads:
        copy.wait()

    def first_block(i, carry):
        for j in range(4):
            first(PAD + 4 * i + j, None)
        return carry

    lax.fori_loop(0, rows // 4, first_block, 0)
    for x in list(range(PAD - GHOST)) + list(range(end + GHOST, end + PAD)):
        inv[x] = jnp.zeros((depth, width), jnp.float32)

    finish(req_r, a2a_rs.at[0])
    slots = jnp.sum(jnp.where(square, req_r[...].astype(jnp.float32), 0.0), axis=2, keepdims=True)
    chosen = (iota((n, cap, init.shape[0]), 2).astype(jnp.float32) == slots).astype(jnp.float32)
    chosen = chosen.reshape(n * cap, init.shape[0])
    choose[...] = chosen.astype(jnp.bfloat16)
    choose_t[...] = chosen.T.astype(jnp.bfloat16)

    wall_s[0] = pick(choose[...], init[...]).reshape(n, cap, width)
    exchange(wall_s.at[0], wall_r.at[0], 1)

    for copy in ghosts:
        copy.wait_recv()
    low_scale = jnp.where(me == 0, 0.0, 1.0)
    high_scale = jnp.where(me == n - 1, 0.0, 1.0)
    for x in range(GHOST):
        first(PAD - GHOST + x, low_scale)
        first(end + x, high_scale)
    for y in range(TOTAL):
        invp[y] = inv[:, y, :]

    row = iota((depth, width), 0)

    def sweep(number):
        old, new = (even, odd) if number % 2 == 1 else (odd, even)
        begin = PAD - (GHOST - number)
        count = rows + 2 * (GHOST - number)

        def planes(x, many):
            held = [old[x - 1 + j] for j in range(many + 2)]
            for j in range(many):
                here = held[j + 1]
                total = src[x + j] + (held[j] + held[j + 2])
                up = jnp.where(row == 0, 0.0, pltpu.roll(here, 1, 0))
                down = jnp.where(row == depth - 1, 0.0, pltpu.roll(here, depth - 1, 0))
                total = total + (up + down) + beside(here)
                new[x + j] = total * inv[x + j]

        def block(i, carry):
            planes(begin + 4 * i, 4)
            return carry

        lax.fori_loop(0, count // 4, block, 0)
        if count % 4:
            planes(begin + count // 4 * 4, count % 4)
        if number % SWEEPS == SWEEPS - 1:
            base[number // SWEEPS] = (
                new[PAD:end, 0, :] - new[PAD:end, 1, :]
            )

    def wall_of(k):
        finish(wall_r.at[k], a2a_rs.at[1 + 2 * k])
        got = wall_r[k].reshape(n * cap, width)
        walls[k, PAD:end, :] = pick(place_t[...], got)
        held = walls.at[k]
        return to_neighbours(
            held.at[pl.ds(PAD, PAD)], held.at[pl.ds(rows, PAD)],
            held.at[pl.ds(0, PAD)], held.at[pl.ds(end, PAD)],
            lambda i: edge_ss.at[k, i], lambda i: edge_rs.at[k, i],
        )

    def change(k, carried):
        wall = walls[k]
        total_rows = wall.shape[0]
        for _ in range(SWEEPS):
            after = []
            for y in range(len(carried) + 1):
                total = wall if y == 0 else None
                terms = []
                if y < len(carried):
                    here = carried[y]
                    terms += [
                        pltpu.roll(here, 1, 0) + pltpu.roll(here, total_rows - 1, 0),
                        beside(here),
                    ]
                if y > 0:
                    terms.append(carried[y - 1])
                if y + 1 < len(carried):
                    terms.append(carried[y + 1])
                for term in terms:
                    total = term if total is None else total + term
                after.append(total * invp[y])
            carried = after
        return carried

    def send_traction(k, carried):
        traction = base[k] + (carried[0] - carried[1])[PAD:end, :]
        trac_s[k] = pick(place[...], traction).reshape(n, cap, width)
        exchange(trac_s.at[k], trac_r.at[k], 2 + 2 * k)

    def solid(k, displacement):
        finish(trac_r.at[k], a2a_rs.at[2 + 2 * k])
        got = trac_r[k].reshape(n * cap, width)
        total = load[...] + pick(choose_t[...], got)
        mismatch = product(total, compliance[...]) - displacement
        part = jnp.sum(jnp.sum(mismatch * mismatch, axis=0, keepdims=True), axis=1, keepdims=True)
        return displacement + RELAX * mismatch, part

    sweep(1)
    sweep(2)
    edges = wall_of(0)
    sweep(3)
    for copy in edges:
        copy.wait_recv()
    carried = change(0, [])
    send_traction(0, carried)
    for y in range(SWEEPS):
        force[y] = carried[y]
    sweep(4)
    displacement, part0 = solid(0, init[...])
    wall_s[1] = pick(choose[...], displacement).reshape(n, cap, width)
    exchange(wall_s.at[1], wall_r.at[1], 3)
    disp_out[...] = displacement
    sweep(5)
    last = odd if GHOST % 2 == 1 else even
    bulk = pltpu.make_async_copy(
        last.at[pl.ds(PAD, rows), pl.ds(PAD, depth - PAD)],
        state_out.at[:, pl.ds(PAD, depth - PAD)],
        out_sem.at[0],
    )
    bulk.start()
    edges2 = wall_of(1)
    for copy in edges2:
        copy.wait_recv()
    carried = change(1, [force[y] for y in range(SWEEPS)])
    send_traction(1, carried)
    for y in range(TOTAL):
        last[PAD:end, y, :] = last[PAD:end, y, :] + carried[y][PAD:end, :]
    top = pltpu.make_async_copy(
        last.at[pl.ds(PAD, rows), pl.ds(0, PAD)],
        state_out.at[:, pl.ds(0, PAD)],
        out_sem.at[1],
    )
    top.start()
    displacement, part1 = solid(1, disp_out[...])
    across = iota((1, width), 1)
    row_of_parts = jnp.where(across == 0, part0, jnp.where(across == 1, part1, 0.0))
    norm_s[...] = jnp.broadcast_to(row_of_parts.reshape(1, 1, width), (n, 1, width))
    exchange(norm_s, norm_r, 5)
    disp_out[...] = displacement

    for copy in ghosts + edges + edges2:
        copy.wait_send()
    finish(req_s, a2a_ss.at[0])
    for k in range(COUPLE):
        finish(wall_s.at[k], a2a_ss.at[1 + 2 * k])
        finish(trac_s.at[k], a2a_ss.at[2 + 2 * k])
    bulk.wait()
    top.wait()
    finish(norm_s, a2a_ss.at[5])
    finish(norm_r, a2a_rs.at[5])
    sums = jnp.sum(norm_r[...], axis=0)
    roots = jnp.sqrt(sums + 1e-06)
    for k in range(COUPLE):
        norm_out[k] = jnp.sum(jnp.where(across == k, roots, 0.0))


def per_device(
    n, dom, fluid_source, coef_ids, coef_table, owner_device, owner_slot,
    solid_init, solid_load, compliance,
):
    rows, depth, width = fluid_source.shape
    solid_rows = solid_init.shape[0]
    tall = rows + 2 * PAD
    f32, bf16 = jnp.float32, jnp.bfloat16
    vmem = pl.BlockSpec(memory_space=pltpu.VMEM)
    smem = pl.BlockSpec(memory_space=pltpu.SMEM)
    anywhere = pl.BlockSpec(memory_space=pl.ANY)
    block = (COUPLE, n, PAD, width)
    return tuple(
        pl.pallas_call(
            functools.partial(kernel, n, dom),
            out_shape=(
                jax.ShapeDtypeStruct((rows, depth, width), f32),
                jax.ShapeDtypeStruct((solid_rows, width), f32),
                jax.ShapeDtypeStruct((COUPLE,), f32),
            ),
            in_specs=[anywhere, anywhere, smem, vmem, vmem, vmem, vmem, vmem],
            out_specs=(anywhere, vmem, smem),
            scratch_shapes=[
                pltpu.VMEM((tall, depth, width), f32),
                pltpu.VMEM((tall, depth, width), jnp.int32),
                pltpu.VMEM((tall, depth, width), f32),
                pltpu.VMEM((tall, depth, width), f32),
                pltpu.VMEM((tall, depth, width), f32),
                pltpu.VMEM((TOTAL, tall, width), f32),
                pltpu.VMEM((COUPLE, rows, width), f32),
                pltpu.VMEM((COUPLE, tall, width), f32),
                pltpu.VMEM((SWEEPS, tall, width), f32),
                pltpu.VMEM((n * PAD, rows), bf16),
                pltpu.VMEM((rows, n * PAD), bf16),
                pltpu.VMEM((n * PAD, solid_rows), bf16),
                pltpu.VMEM((solid_rows, n * PAD), bf16),
                pltpu.VMEM((n, 1, width), jnp.int32),
                pltpu.VMEM((n, 1, width), jnp.int32),
                pltpu.VMEM(block, f32),
                pltpu.VMEM(block, f32),
                pltpu.VMEM(block, f32),
                pltpu.VMEM(block, f32),
                pltpu.VMEM((n, 1, width), f32),
                pltpu.VMEM((n, 1, width), f32),
                pltpu.SemaphoreType.DMA((2,)),
                pltpu.SemaphoreType.DMA((2,)),
                pltpu.SemaphoreType.DMA((2, 2)),
                pltpu.SemaphoreType.DMA((2, 2)),
                pltpu.SemaphoreType.DMA((2 + 2 * COUPLE,)),
                pltpu.SemaphoreType.DMA((2 + 2 * COUPLE,)),
                pltpu.SemaphoreType.DMA((COUPLE, 2)),
                pltpu.SemaphoreType.DMA((COUPLE, 2)),
            ],
            compiler_params=pltpu.CompilerParams(
                collective_id=0, has_side_effects=True, vmem_limit_bytes=48 * 2**20
            ),
        )(
            fluid_source, coef_ids, coef_table,
            owner_device.reshape(1, rows), owner_slot.reshape(1, rows),
            solid_init, solid_load, compliance,
        )
    )


def solution(mesh):
    rows = P(("sect", "dom"), None)
    cells = P(("sect", "dom"), None, None)
    n = mesh.shape["sect"] * mesh.shape["dom"]
    return jax.shard_map(
        functools.partial(per_device, n, mesh.shape["dom"]),
        mesh=mesh,
        in_specs=(cells, cells, P(), rows, rows, rows, rows, P()),
        out_specs=(cells, rows, P()),
        check_vma=False,
    )
```

time: 270 us -> 62.3 us (0.23)
  blocking collectives: 105 us -> 0 us
  other arithmetic: 101 us -> 0 us
  Pallas kernels: 0 us -> 52.8 us
  starting transfers between devices: 33.4 us -> 0 us
  waiting for transfers between devices: 7.84 us -> 0 us
  local copies, waits for them, and re-layouts: 14 us -> 8.53 us
  matrix products: 5.28 us -> 0 us
    div x6 -> x0, other arithmetic: 98.1 us -> none  [per_device(): fluid_state = (source + neighbours(padded)) / diagonal]
    all_to_all x3 -> x0, blocking collectives: 66.8 us -> none  [the longest x2 52.6 us: route_traction(): lax.all_to_all(buffer, ('sect', 'dom'), split_axis=0, concat_axis=0, tile...]
    pallas_call x0 -> x1, Pallas kernels: none -> 52.8 us  [per_device(): pl.pallas_call(functools.partial(kernel, n, dom), out_shape=(jax.ShapeDty...]
    psum x1 -> x0, blocking collectives: 38.3 us -> none  [per_device(): totals = lax.psum(jnp.stack(partials), ('sect', 'dom'))]
    ppermute x12 -> x0, starting transfers between devices: 28.3 us -> none  [the longest x6 20.6 us: with_halo(): lax.ppermute(lax.slice_in_dim(block, block.shape[dim] - width, None, axis...]
    scatter-add x2 -> x0, local copies, waits for them, and re-layouts: 5.9 us -> none  [per_device(): source = fluid_source.at[:, 0, :].add(wall_rows)]
    dot_general x10 -> x0, matrix products: 5.28 us -> none  [the longest x2 1.81 us: per_device(): answer = jnp.dot(picker, displacement, precision=highest)]
    all_to_all x2 -> x0, starting transfers between devices: 5.11 us -> none  [route_wall(): lax.all_to_all(buffer, ('sect', 'dom'), split_axis=0, concat_axis=0, tile...]
  transfers between devices with their start and end apart: 14 -> 0, of which waited for: 6 -> 0; matrix products, arithmetic and copies ran while one was open for 3% -> 0% of each run, Pallas kernels for 0% -> 0%
where the time goes in v1:
time: 62.3 us; the launch traced here: 62 us
  Pallas kernels  52.8 us (85%)
  local copies, waits for them, and re-layouts  8.53 us (14%)
  between operations  0.66 us (1%)
    pallas_call x1, Pallas kernels, per_device(): pl.pallas_call(functools.partial(kernel, n, dom), out_shape=(jax.ShapeDty...  52.8 us
    unnamed x17, local copies, waits for them, and re-layouts  8.53 us

profile of v1, /device:TPU:0, one launch (start us, length us, event | category | flops | bytes accessed | tf_op | source)
XLA Modules:
  0.0 62.0 jit_solution(17567795606136840976)
XLA Ops:
  0.6 0.0 copy-start
  0.6 1.6 %copy-done = f32[128,32,128]{2,1,0:T(8,128)S(1)} copy-done((f32[128,32,128]{2,1,0:T(8,128)S(1)}, f32[128,32,128]{2,1,0:T(8,128)}, u32[]{:S(2)}) %copy-start) | copy-done | bytes 2097176
  2.2 0.0 copy-start.1
  2.2 0.8 %copy-done.1 = f32[128,128]{1,0:T(8,128)S(1)} copy-done((f32[128,128]{1,0:T(8,128)S(1)}, f32[128,128]{1,0:T(8,128)}, u32[]{:S(2)}) %copy-start.1) | copy-done | bytes 65560
  3.1 0.0 copy-start.2
  3.1 0.8 %copy-done.2 = f32[128,128]{1,0:T(8,128)S(1)} copy-done((f32[128,128]{1,0:T(8,128)S(1)}, f32[128,128]{1,0:T(8,128)}, u32[]{:S(2)}) %copy-start.2) | copy-done | bytes 65560
  3.9 0.0 copy-start.3
  3.9 0.8 %copy-done.3 = f32[128,128]{1,0:T(8,128)S(1)} copy-done((f32[128,128]{1,0:T(8,128)S(1)}, f32[128,128]{1,0:T(8,128)}, u32[]{:S(2)}) %copy-start.3) | copy-done | bytes 65560
  4.7 0.0 copy-start.4
  4.7 0.7 %copy-done.4 = f32[16]{0:T(128)S(1)} copy-done((f32[16]{0:T(128)S(1)}, f32[16]{0:T(128)}, u32[]{:S(2)}) %copy-start.4) | copy-done | bytes 88
  5.4 0.0 copy-start.5
  5.4 0.7 %copy-done.5 = s32[128,1]{0,1:T(1,128)S(1)} copy-done((s32[128,1]{0,1:T(1,128)S(1)}, s32[128,1]{0,1:T(1,128)}, u32[]{:S(2)}) %copy-start.5) | copy-done | bytes 536
  6.1 0.0 copy-start.6
  6.1 0.7 %copy-done.6 = s32[128,1]{0,1:T(1,128)S(1)} copy-done((s32[128,1]{0,1:T(1,128)S(1)}, s32[128,1]{0,1:T(1,128)}, u32[]{:S(2)}) %copy-start.6) | copy-done | bytes 536
  6.7 52.8 %shard_map.103 = (f32[128,32,128]{2,1,0:T(8,128)S(1)}, f32[128,128]{1,0:T(8,128)S(1)}, f32[2]{0:T(128)S(1)}) custom-call(f32[128,32,128]{2,1,0:T(8,128)S(1)} %copy-done, s32[128,32,128]{2,1,0:T(8,128)} %ids.1, f32[16]{0:T(128)S(1)} %copy-done.4, s32[1,128]{1,0:T(1,128)S(1)} %bitcast.2, s32[1,128]{1,0:T(1,128)S(1)} %bitcast.3, f32[128,128]{1,0:T(8,128)S(1)} %copy-done.1, ...), custom_call_target="tpu_custom_call" | custom-call | tf_op jit(solution)/shard_map/pallas_call | solution.py:343
  59.5 1.3 %copy.14 = f32[128,32,128]{2,1,0:T(8,128)} copy(f32[128,32,128]{2,1,0:T(8,128)S(1)} %get-tuple-element.6) | data formatting | bytes 4194304
  60.9 0.6 %copy.15 = f32[128,128]{1,0:T(8,128)} copy(f32[128,128]{1,0:T(8,128)S(1)} %get-tuple-element.7) | data formatting | bytes 131072
  61.5 0.5 copy.16
Async XLA Ops:
  0.6 1.6 %copy-start = (f32[128,32,128]{2,1,0:T(8,128)S(1)}, f32[128,32,128]{2,1,0:T(8,128)}, u32[]{:S(2)}) copy-start(f32[128,32,128]{2,1,0:T(8,128)} %source.1) | copy-start | bytes 6291460
  2.2 0.8 %copy-start.1 = (f32[128,128]{1,0:T(8,128)S(1)}, f32[128,128]{1,0:T(8,128)}, u32[]{:S(2)}) copy-start(f32[128,128]{1,0:T(8,128)} %init.1) | copy-start | bytes 196612
  3.1 0.8 %copy-start.2 = (f32[128,128]{1,0:T(8,128)S(1)}, f32[128,128]{1,0:T(8,128)}, u32[]{:S(2)}) copy-start(f32[128,128]{1,0:T(8,128)} %load.1) | copy-start | bytes 196612
  3.9 0.8 %copy-start.3 = (f32[128,128]{1,0:T(8,128)S(1)}, f32[128,128]{1,0:T(8,128)}, u32[]{:S(2)}) copy-start(f32[128,128]{1,0:T(8,128)} %compliance.1) | copy-start | bytes 196612
  4.7 0.7 %copy-start.4 = (f32[16]{0:T(128)S(1)}, f32[16]{0:T(128)}, u32[]{:S(2)}) copy-start(f32[16]{0:T(128)} %table.1) | copy-start | bytes 196
  5.4 0.7 %copy-start.5 = (s32[128,1]{0,1:T(1,128)S(1)}, s32[128,1]{0,1:T(1,128)}, u32[]{:S(2)}) copy-start(s32[128,1]{0,1:T(1,128)} %param.11) | copy-start | bytes 1540
  6.1 0.7 %copy-start.6 = (s32[128,1]{0,1:T(1,128)S(1)}, s32[128,1]{0,1:T(1,128)}, u32[]{:S(2)}) copy-start(s32[128,1]{0,1:T(1,128)} %param.12) | copy-start | bytes 1540

commit v2 on v1

--- a/solution.py
+++ b/solution.py
@@ -13,6 +13,7 @@
 TOTAL = SWEEPS * COUPLE
 GHOST = TOTAL - 1
 PAD = 8
+VMEM = 58 * 2**20
 MESH = pl.DeviceIdType.MESH
 
 
@@ -50,9 +51,10 @@
 
 
 def kernel(
-    n, dom, source, ids, table, owner, slot, init, load, compliance,
+    n, dom, source, ids, table_in, owner_in, slot_in, init_in, load_in, compliance_in,
     state_out, disp_out, norm_out,
-    src, idv, inv, even, odd, invp, base, walls, force,
+    table, owner, slot, init, load, compliance,
+    src, idv, inv, even, odd, invp, base, walls, force, trac, disp,
     place, place_t, choose, choose_t,
     req_s, req_r, wall_s, wall_r, trac_s, trac_r, norm_s, norm_r,
     in_sem, out_sem, ghost_ss, ghost_rs, a2a_ss, a2a_rs, edge_ss, edge_rs,
@@ -60,30 +62,53 @@
     rows, depth, width = source.shape
     end = PAD + rows
     cap = PAD
-    me = lax.axis_index("sect") * dom + lax.axis_index("dom")
-
-    def coords(index):
-        return (lax.div(index, dom), lax.rem(index, dom))
-
-    right = coords(lax.rem(me + 1, n))
-    left = coords(lax.rem(me + n - 1, n))
+    sect = n // dom
+    my_sect, my_dom = lax.axis_index("sect"), lax.axis_index("dom")
+    me = my_sect * dom + my_dom
+
+    def after(sect_at, dom_at):
+        over = dom_at + 1 == dom
+        dom_next = jnp.where(over, 0, dom_at + 1)
+        sect_next = jnp.where(over, sect_at + 1, sect_at)
+        return jnp.where(sect_next == sect, 0, sect_next), dom_next
+
+    def ahead(sect_at, dom_at):
+        under = dom_at == 0
+        dom_next = jnp.where(under, dom - 1, dom_at - 1)
+        sect_next = jnp.where(under, sect_at - 1, sect_at)
+        return jnp.where(sect_next < 0, sect - 1, sect_next), dom_next
+
+    right = after(my_sect, my_dom)
+    left = ahead(my_sect, my_dom)
+
+    def each_peer(act):
+        def one(k, at):
+            act(*at)
+            return after(*at)
+
+        beyond = jnp.where(my_sect + 1 == sect, 0, my_sect + 1)
+        at = lax.fori_loop(0, n - dom, one, (beyond, my_dom))
+        lax.fori_loop(1, dom, one, after(*at))
 
     loads = [
-        pltpu.make_async_copy(source, src.at[pl.ds(PAD, rows)], in_sem.at[0]),
-        pltpu.make_async_copy(ids, idv.at[pl.ds(PAD, rows)], in_sem.at[1]),
+        pltpu.make_async_copy(a, b, in_sem.at[i])
+        for i, (a, b) in enumerate((
+            (owner_in, owner), (slot_in, slot), (table_in, table),
+            (ids, idv.at[pl.ds(PAD, rows)]), (source, src.at[pl.ds(PAD, rows)]),
+            (init_in, init), (load_in, load), (compliance_in, compliance),
+        ))
     ]
-    for copy in loads:
+    for copy in loads[:2]:
         copy.start()
 
     barrier = pltpu.get_barrier_semaphore()
-
-    def greet(k, carry):
-        pl.semaphore_signal(
-            barrier, inc=1, device_id=coords(lax.rem(me + k, n)), device_id_type=MESH
-        )
-        return carry
-
-    lax.fori_loop(1, n, greet, 0)
+    each_peer(lambda *at: pl.semaphore_signal(
+        barrier, inc=1, device_id=at, device_id_type=MESH
+    ))
+    for copy in loads[2:]:
+        copy.start()
+    for copy in loads[:2]:
+        copy.wait()
 
     owner_row = owner[...]
     slot_row = slot[...]
@@ -103,19 +128,17 @@
     pl.semaphore_wait(barrier, n - 1)
 
     def exchange(sent, got, phase):
-        def one(k, carry):
-            peer = lax.rem(me + k, n)
+        def one(sect_at, dom_at):
             pltpu.make_async_remote_copy(
-                src_ref=sent.at[peer],
+                src_ref=sent.at[sect_at * dom + dom_at],
                 dst_ref=got.at[me],
                 send_sem=a2a_ss.at[phase],
                 recv_sem=a2a_rs.at[phase],
-                device_id=coords(peer),
+                device_id=(sect_at, dom_at),
                 device_id_type=MESH,
             ).start()
-            return carry
-
-        lax.fori_loop(1, n, one, 0)
+
+        each_peer(one)
         got[me] = sent[me]
 
     def finish(ref, sem):
@@ -146,6 +169,9 @@
             lambda i: ghost_ss.at[number, i], lambda i: ghost_rs.at[number, i],
         )
 
+    for copy in loads[2:]:
+        copy.wait()
+
     lane = iota((depth, width), 1)
     recip = jnp.zeros((depth, width), jnp.float32)
     for entry in range(table.shape[0]):
@@ -158,9 +184,6 @@
             value = value * scale
         inv[x] = value
         even[x] = src[x] * value
-
-    for copy in loads:
-        copy.wait()
 
     def first_block(i, carry):
         for j in range(4):
@@ -223,42 +246,70 @@
     def wall_of(k):
         finish(wall_r.at[k], a2a_rs.at[1 + 2 * k])
         got = wall_r[k].reshape(n * cap, width)
-        walls[k, PAD:end, :] = pick(place_t[...], got)
+        mine = pick(place_t[...], got)
+        walls[k, PAD:end, :] = mine
         held = walls.at[k]
-        return to_neighbours(
+        return mine, to_neighbours(
             held.at[pl.ds(PAD, PAD)], held.at[pl.ds(rows, PAD)],
             held.at[pl.ds(0, PAD)], held.at[pl.ds(end, PAD)],
             lambda i: edge_ss.at[k, i], lambda i: edge_rs.at[k, i],
         )
 
-    def change(k, carried):
-        wall = walls[k]
-        total_rows = wall.shape[0]
-        for _ in range(SWEEPS):
-            after = []
-            for y in range(len(carried) + 1):
-                total = wall if y == 0 else None
-                terms = []
-                if y < len(carried):
-                    here = carried[y]
-                    terms += [
-                        pltpu.roll(here, 1, 0) + pltpu.roll(here, total_rows - 1, 0),
-                        beside(here),
-                    ]
+    def spread(wall, begun, factor):
+        found = {}
+
+        def plane(step, y):
+            if y >= len(begun) + step:
+                return None
+            if step == 0:
+                return begun[y]
+            if (step, y) not in found:
+                terms = [wall] if y == 0 else []
+                here = plane(step - 1, y)
+                if here is not None:
+                    tall = here.shape[0]
+                    terms.append(pltpu.roll(here, 1, 0) + pltpu.roll(here, tall - 1, 0))
+                    terms.append(beside(here))
                 if y > 0:
-                    terms.append(carried[y - 1])
-                if y + 1 < len(carried):
-                    terms.append(carried[y + 1])
-                for term in terms:
-                    total = term if total is None else total + term
-                after.append(total * invp[y])
-            carried = after
-        return carried
-
-    def send_traction(k, carried):
-        traction = base[k] + (carried[0] - carried[1])[PAD:end, :]
-        trac_s[k] = pick(place[...], traction).reshape(n, cap, width)
+                    terms.append(plane(step - 1, y - 1))
+                terms.append(plane(step - 1, y + 1))
+                terms = [term for term in terms if term is not None]
+                found[step, y] = functools.reduce(jnp.add, terms) * factor(y)
+            return found[step, y]
+
+        return plane
+
+    def iterate(k, begun):
+        mine, edges = wall_of(k)
+        margin = jnp.zeros((PAD, width), jnp.float32)
+        own = spread(jnp.concatenate([margin, mine, margin], axis=0), begun, lambda y: invp[y])
+        traction = base[k] + (own(SWEEPS, 0) - own(SWEEPS, 1))[PAD:end, :]
+        trac[...] = traction
+        for copy in edges:
+            copy.wait_recv()
+
+        outer = jnp.concatenate(
+            [walls[k, :PAD, :], margin, margin, walls[k, end:, :]], axis=0
+        )
+        other = spread(outer, [], lambda y: jnp.concatenate(
+            [invp[y, :2 * PAD, :], invp[y, end - PAD:, :]], axis=0
+        ))
+        jump = other(SWEEPS, 0) - other(SWEEPS, 1)
+        trac[:PAD, :] = trac[:PAD, :] + jump[PAD:2 * PAD, :]
+        trac[rows - PAD:, :] = trac[rows - PAD:, :] + jump[2 * PAD:3 * PAD, :]
+        trac_s[k] = pick(place[...], trac[...]).reshape(n, cap, width)
         exchange(trac_s.at[k], trac_r.at[k], 2 + 2 * k)
+        middle = jnp.zeros((rows - 2 * PAD, width), jnp.float32)
+        planes = []
+        for y in range(len(begun) + SWEEPS):
+            total = own(SWEEPS, y)
+            if y < SWEEPS:
+                share = other(SWEEPS, y)
+                total = total + jnp.concatenate(
+                    [share[:2 * PAD, :], middle, share[2 * PAD:, :]], axis=0
+                )
+            planes.append(total)
+        return planes, edges
 
     def solid(k, displacement):
         finish(trac_r.at[k], a2a_rs.at[2 + 2 * k])
@@ -270,19 +321,15 @@
 
     sweep(1)
     sweep(2)
-    edges = wall_of(0)
+    planes, edges = iterate(0, [])
+    for y in range(SWEEPS):
+        force[y] = planes[y]
     sweep(3)
-    for copy in edges:
-        copy.wait_recv()
-    carried = change(0, [])
-    send_traction(0, carried)
-    for y in range(SWEEPS):
-        force[y] = carried[y]
     sweep(4)
     displacement, part0 = solid(0, init[...])
     wall_s[1] = pick(choose[...], displacement).reshape(n, cap, width)
     exchange(wall_s.at[1], wall_r.at[1], 3)
-    disp_out[...] = displacement
+    disp[...] = displacement
     sweep(5)
     last = odd if GHOST % 2 == 1 else even
     bulk = pltpu.make_async_copy(
@@ -291,25 +338,23 @@
         out_sem.at[0],
     )
     bulk.start()
-    edges2 = wall_of(1)
-    for copy in edges2:
-        copy.wait_recv()
-    carried = change(1, [force[y] for y in range(SWEEPS)])
-    send_traction(1, carried)
+    planes, edges2 = iterate(1, [force[y] for y in range(SWEEPS)])
     for y in range(TOTAL):
-        last[PAD:end, y, :] = last[PAD:end, y, :] + carried[y][PAD:end, :]
+        last[PAD:end, y, :] = last[PAD:end, y, :] + planes[y][PAD:end, :]
     top = pltpu.make_async_copy(
         last.at[pl.ds(PAD, rows), pl.ds(0, PAD)],
         state_out.at[:, pl.ds(0, PAD)],
         out_sem.at[1],
     )
     top.start()
-    displacement, part1 = solid(1, disp_out[...])
+    displacement, part1 = solid(1, disp[...])
     across = iota((1, width), 1)
     row_of_parts = jnp.where(across == 0, part0, jnp.where(across == 1, part1, 0.0))
     norm_s[...] = jnp.broadcast_to(row_of_parts.reshape(1, 1, width), (n, 1, width))
     exchange(norm_s, norm_r, 5)
-    disp_out[...] = displacement
+    disp[...] = displacement
+    moved = pltpu.make_async_copy(disp, disp_out, out_sem.at[2])
+    moved.start()
 
     for copy in ghosts + edges + edges2:
         copy.wait_send()
@@ -319,12 +364,30 @@
         finish(trac_s.at[k], a2a_ss.at[2 + 2 * k])
     bulk.wait()
     top.wait()
+    moved.wait()
     finish(norm_s, a2a_ss.at[5])
     finish(norm_r, a2a_rs.at[5])
-    sums = jnp.sum(norm_r[...], axis=0)
-    roots = jnp.sqrt(sums + 1e-06)
+    norm_out[...] = jnp.sum(norm_r[...], axis=0)
+
+
+def store_kernel(state, disp, sums, state_out, disp_out, norm_out, held, sem):
+    parts = 8
+    arrive = pltpu.make_async_copy(sums, held, sem.at[parts + 1])
+    arrive.start()
+    rows = state.shape[0] // parts
+    copies = [pltpu.make_async_copy(disp, disp_out, sem.at[parts])]
+    for i in range(parts):
+        part = pl.ds(i * rows, rows)
+        copies.append(pltpu.make_async_copy(state.at[part], state_out.at[part], sem.at[i]))
+    for copy in copies:
+        copy.start()
+    arrive.wait()
+    roots = jnp.sqrt(held[...] + 1e-06)
+    across = iota(roots.shape, 1)
     for k in range(COUPLE):
         norm_out[k] = jnp.sum(jnp.where(across == k, roots, 0.0))
+    for copy in copies:
+        copy.wait()
 
 
 def per_device(
@@ -337,19 +400,25 @@
     f32, bf16 = jnp.float32, jnp.bfloat16
     vmem = pl.BlockSpec(memory_space=pltpu.VMEM)
     smem = pl.BlockSpec(memory_space=pltpu.SMEM)
-    anywhere = pl.BlockSpec(memory_space=pl.ANY)
+    hbm = pl.BlockSpec(memory_space=pltpu.HBM)
     block = (COUPLE, n, PAD, width)
-    return tuple(
+    state, disp, sums = (
         pl.pallas_call(
             functools.partial(kernel, n, dom),
             out_shape=(
                 jax.ShapeDtypeStruct((rows, depth, width), f32),
                 jax.ShapeDtypeStruct((solid_rows, width), f32),
-                jax.ShapeDtypeStruct((COUPLE,), f32),
+                jax.ShapeDtypeStruct((1, width), f32),
             ),
-            in_specs=[anywhere, anywhere, smem, vmem, vmem, vmem, vmem, vmem],
-            out_specs=(anywhere, vmem, smem),
+            in_specs=[hbm] * 8,
+            out_specs=(hbm, hbm, vmem),
             scratch_shapes=[
+                pltpu.SMEM(coef_table.shape, f32),
+                pltpu.VMEM((1, rows), jnp.int32),
+                pltpu.VMEM((1, rows), jnp.int32),
+                pltpu.VMEM((solid_rows, width), f32),
+                pltpu.VMEM((solid_rows, width), f32),
+                pltpu.VMEM((width, width), f32),
                 pltpu.VMEM((tall, depth, width), f32),
                 pltpu.VMEM((tall, depth, width), jnp.int32),
                 pltpu.VMEM((tall, depth, width), f32),
@@ -359,6 +428,8 @@
                 pltpu.VMEM((COUPLE, rows, width), f32),
                 pltpu.VMEM((COUPLE, tall, width), f32),
                 pltpu.VMEM((SWEEPS, tall, width), f32),
+                pltpu.VMEM((rows, width), f32),
+                pltpu.VMEM((solid_rows, width), f32),
                 pltpu.VMEM((n * PAD, rows), bf16),
                 pltpu.VMEM((rows, n * PAD), bf16),
                 pltpu.VMEM((n * PAD, solid_rows), bf16),
@@ -371,8 +442,8 @@
                 pltpu.VMEM(block, f32),
                 pltpu.VMEM((n, 1, width), f32),
                 pltpu.VMEM((n, 1, width), f32),
-                pltpu.SemaphoreType.DMA((2,)),
-                pltpu.SemaphoreType.DMA((2,)),
+                pltpu.SemaphoreType.DMA((8,)),
+                pltpu.SemaphoreType.DMA((3,)),
                 pltpu.SemaphoreType.DMA((2, 2)),
                 pltpu.SemaphoreType.DMA((2, 2)),
                 pltpu.SemaphoreType.DMA((2 + 2 * COUPLE,)),
@@ -381,13 +452,27 @@
                 pltpu.SemaphoreType.DMA((COUPLE, 2)),
             ],
             compiler_params=pltpu.CompilerParams(
-                collective_id=0, has_side_effects=True, vmem_limit_bytes=48 * 2**20
+                collective_id=0, has_side_effects=True, vmem_limit_bytes=VMEM
             ),
         )(
             fluid_source, coef_ids, coef_table,
             owner_device.reshape(1, rows), owner_slot.reshape(1, rows),
             solid_init, solid_load, compliance,
         )
+    )
+    return tuple(
+        pl.pallas_call(
+            store_kernel,
+            out_shape=(
+                jax.ShapeDtypeStruct(state.shape, f32),
+                jax.ShapeDtypeStruct(disp.shape, f32),
+                jax.ShapeDtypeStruct((COUPLE,), f32),
+            ),
+            in_specs=[hbm] * 3,
+            out_specs=(hbm, hbm, smem),
+            scratch_shapes=[pltpu.VMEM(sums.shape, f32), pltpu.SemaphoreType.DMA((10,))],
+            compiler_params=pltpu.CompilerParams(vmem_limit_bytes=VMEM),
+        )(state, disp, sums)
     )
 
 

time: 62.3 us -> 123 us (1.97)
  Pallas kernels: 52.8 us -> 122 us
  local copies, waits for them, and re-layouts: 8.53 us -> 0 us
    pallas_call x0 -> x1, Pallas kernels: none -> 67.2 us  [per_device(): pl.pallas_call(store_kernel, out_shape=(jax.ShapeDtypeStruct(state.shape,...]
    unnamed x17 -> x0, local copies, waits for them, and re-layouts: 8.53 us -> none
    pallas_call x1, Pallas kernels: 52.8 us -> 55.2 us  [per_device(): pl.pallas_call(functools.partial(kernel, n, dom), out_shape=(jax.ShapeDty...]
where the time goes in v2:
time: 123 us
  Pallas kernels  122 us (99%)
    pallas_call x1, Pallas kernels, per_device(): pl.pallas_call(store_kernel, out_shape=(jax.ShapeDtypeStruct(state.shape,...  67.2 us
    pallas_call x1, Pallas kernels, per_device(): pl.pallas_call(functools.partial(kernel, n, dom), out_shape=(jax.ShapeDty...  55.2 us

profile of v2, /device:TPU:0, one launch (start us, length us, event | category | flops | bytes accessed | tf_op | source)
XLA Modules:
  0.0 123.0 jit_solution(2742967275270546294)
XLA Ops:
  0.6 55.2 %shard_map.103 = (f32[128,32,128]{2,1,0:T(8,128)}, f32[128,128]{1,0:T(8,128)}, f32[1,128]{1,0:T(1,128)}) custom-call(f32[128,32,128]{2,1,0:T(8,128)} %source.1, s32[128,32,128]{2,1,0:T(8,128)} %ids.1, f32[16]{0:T(128)} %table_in.1, s32[1,128]{1,0:T(1,128)} %bitcast.2, s32[1,128]{1,0:T(1,128)} %bitcast.3, f32[128,128]{1,0:T(8,128)} %init_in.1, ...), custom_call_target="tpu_custom_call" | custom-call | tf_op jit(solution)/shard_map/pallas_call | solution.py:406
  55.8 67.2 %shard_map.104 = (f32[128,32,128]{2,1,0:T(8,128)}, f32[128,128]{1,0:T(8,128)}, f32[2]{0:T(128)}) custom-call(f32[128,32,128]{2,1,0:T(8,128)} %get-tuple-element.6.state, f32[128,128]{1,0:T(8,128)} %get-tuple-element.7.disp, f32[1,128]{1,0:T(1,128)} %get-tuple-element.8.sums), custom_call_target="tpu_custom_call" | custom-call | tf_op jit(solution)/shard_map/pallas_call | solution.py:464

commit v3 on v2

--- a/solution.py
+++ b/solution.py
@@ -119,12 +119,33 @@
     position = owner_row * cap + rank
     placed = (iota((n * cap, rows), 0) == position).astype(jnp.float32)
     place[...] = placed.astype(jnp.bfloat16)
-    place_t[...] = placed.T.astype(jnp.bfloat16)
     wanted = jnp.sum(placed * (slot_row + 1).astype(jnp.float32), axis=1, keepdims=True) - 1.0
     wanted = wanted.reshape(n, cap, 1)
     square = iota((n, cap, width), 2) == iota((n, cap, width), 1)
     req_s[...] = jnp.sum(jnp.where(square, wanted, 0.0), axis=1, keepdims=True).astype(jnp.int32)
 
+    for copy in loads[2:]:
+        copy.wait()
+
+    lane = iota((depth, width), 1)
+    recip = jnp.zeros((depth, width), jnp.float32)
+    for entry in range(table.shape[0]):
+        recip = jnp.where(lane == entry, table[entry], recip)
+    recip = 1.0 / (6.0 + recip)
+
+    def first(x, scale):
+        value = jnp.take_along_axis(recip, idv[x], axis=1, mode="promise_in_bounds")
+        if scale is not None:
+            value = value * scale
+        inv[x] = value
+        even[x] = src[x] * value
+
+    def first_block(i, carry):
+        for j in range(4):
+            first(PAD + 4 * i + j, None)
+        return carry
+
+    lax.fori_loop(0, rows // 4, first_block, 0)
     pl.semaphore_wait(barrier, n - 1)
 
     def exchange(sent, got, phase):
@@ -146,6 +167,7 @@
         pltpu.make_async_copy(part, part, sem).wait()
 
     exchange(req_s, req_r, 0)
+    place_t[...] = placed.T.astype(jnp.bfloat16)
 
     def to_neighbours(from_low, from_high, to_low, to_high, ss, rs):
         copies = [
@@ -169,40 +191,50 @@
             lambda i: ghost_ss.at[number, i], lambda i: ghost_rs.at[number, i],
         )
 
-    for copy in loads[2:]:
-        copy.wait()
-
-    lane = iota((depth, width), 1)
-    recip = jnp.zeros((depth, width), jnp.float32)
-    for entry in range(table.shape[0]):
-        recip = jnp.where(lane == entry, table[entry], recip)
-    recip = 1.0 / (6.0 + recip)
-
-    def first(x, scale):
-        value = jnp.take_along_axis(recip, idv[x], axis=1, mode="promise_in_bounds")
-        if scale is not None:
-            value = value * scale
-        inv[x] = value
-        even[x] = src[x] * value
-
-    def first_block(i, carry):
-        for j in range(4):
-            first(PAD + 4 * i + j, None)
-        return carry
-
-    lax.fori_loop(0, rows // 4, first_block, 0)
+    row = iota((depth, width), 0)
+
+    def sweep(number, begin, stop):
+        old, new = (even, odd) if number % 2 == 1 else (odd, even)
+        count = stop - begin
+
+        def planes(x, many):
+            held = [old[x - 1 + j] for j in range(many + 2)]
+            for j in range(many):
+                here = held[j + 1]
+                total = src[x + j] + (held[j] + held[j + 2])
+                up = jnp.where(row == 0, 0.0, pltpu.roll(here, 1, 0))
+                down = jnp.where(row == depth - 1, 0.0, pltpu.roll(here, depth - 1, 0))
+                total = total + (up + down) + beside(here)
+                new[x + j] = total * inv[x + j]
+
+        def block(i, carry):
+            planes(begin + 4 * i, 4)
+            return carry
+
+        lax.fori_loop(0, count // 4, block, 0)
+        if count % 4:
+            planes(begin + count // 4 * 4, count % 4)
+
+    def whole(number):
+        sweep(number, PAD - (GHOST - number), end + (GHOST - number))
+
+    def tractions(number):
+        new = odd if number % 2 == 1 else even
+        base[number // SWEEPS] = new[PAD:end, 0, :] - new[PAD:end, 1, :]
+
     for x in list(range(PAD - GHOST)) + list(range(end + GHOST, end + PAD)):
         inv[x] = jnp.zeros((depth, width), jnp.float32)
+
+    sweep(1, PAD + 1, end - 1)
 
     finish(req_r, a2a_rs.at[0])
     slots = jnp.sum(jnp.where(square, req_r[...].astype(jnp.float32), 0.0), axis=2, keepdims=True)
     chosen = (iota((n, cap, init.shape[0]), 2).astype(jnp.float32) == slots).astype(jnp.float32)
     chosen = chosen.reshape(n * cap, init.shape[0])
     choose[...] = chosen.astype(jnp.bfloat16)
-    choose_t[...] = chosen.T.astype(jnp.bfloat16)
-
     wall_s[0] = pick(choose[...], init[...]).reshape(n, cap, width)
     exchange(wall_s.at[0], wall_r.at[0], 1)
+    choose_t[...] = chosen.T.astype(jnp.bfloat16)
 
     for copy in ghosts:
         copy.wait_recv()
@@ -213,35 +245,6 @@
         first(end + x, high_scale)
     for y in range(TOTAL):
         invp[y] = inv[:, y, :]
-
-    row = iota((depth, width), 0)
-
-    def sweep(number):
-        old, new = (even, odd) if number % 2 == 1 else (odd, even)
-        begin = PAD - (GHOST - number)
-        count = rows + 2 * (GHOST - number)
-
-        def planes(x, many):
-            held = [old[x - 1 + j] for j in range(many + 2)]
-            for j in range(many):
-                here = held[j + 1]
-                total = src[x + j] + (held[j] + held[j + 2])
-                up = jnp.where(row == 0, 0.0, pltpu.roll(here, 1, 0))
-                down = jnp.where(row == depth - 1, 0.0, pltpu.roll(here, depth - 1, 0))
-                total = total + (up + down) + beside(here)
-                new[x + j] = total * inv[x + j]
-
-        def block(i, carry):
-            planes(begin + 4 * i, 4)
-            return carry
-
-        lax.fori_loop(0, count // 4, block, 0)
-        if count % 4:
-            planes(begin + count // 4 * 4, count % 4)
-        if number % SWEEPS == SWEEPS - 1:
-            base[number // SWEEPS] = (
-                new[PAD:end, 0, :] - new[PAD:end, 1, :]
-            )
 
     def wall_of(k):
         finish(wall_r.at[k], a2a_rs.at[1 + 2 * k])
@@ -316,21 +319,28 @@
         got = trac_r[k].reshape(n * cap, width)
         total = load[...] + pick(choose_t[...], got)
         mismatch = product(total, compliance[...]) - displacement
-        part = jnp.sum(jnp.sum(mismatch * mismatch, axis=0, keepdims=True), axis=1, keepdims=True)
-        return displacement + RELAX * mismatch, part
-
-    sweep(1)
-    sweep(2)
+        return displacement + RELAX * mismatch, mismatch
+
+    def squares(mismatch):
+        return jnp.sum(jnp.sum(mismatch * mismatch, axis=0, keepdims=True), axis=1, keepdims=True)
+
+    sweep(1, PAD - GHOST + 1, PAD + 1)
+    sweep(1, end - 1, end + GHOST - 1)
+    whole(2)
+    tractions(2)
     planes, edges = iterate(0, [])
     for y in range(SWEEPS):
         force[y] = planes[y]
-    sweep(3)
-    sweep(4)
-    displacement, part0 = solid(0, init[...])
+    whole(3)
+    sweep(4, PAD - 1, PAD + rows // 2)
+    displacement, mismatch = solid(0, init[...])
     wall_s[1] = pick(choose[...], displacement).reshape(n, cap, width)
     exchange(wall_s.at[1], wall_r.at[1], 3)
     disp[...] = displacement
-    sweep(5)
+    part0 = squares(mismatch)
+    sweep(4, PAD + rows // 2, end + 1)
+    whole(5)
+    tractions(5)
     last = odd if GHOST % 2 == 1 else even
     bulk = pltpu.make_async_copy(
         last.at[pl.ds(PAD, rows), pl.ds(PAD, depth - PAD)],
@@ -347,7 +357,8 @@
         out_sem.at[1],
     )
     top.start()
-    displacement, part1 = solid(1, disp[...])
+    displacement, mismatch = solid(1, disp[...])
+    part1 = squares(mismatch)
     across = iota((1, width), 1)
     row_of_parts = jnp.where(across == 0, part0, jnp.where(across == 1, part1, 0.0))
     norm_s[...] = jnp.broadcast_to(row_of_parts.reshape(1, 1, width), (n, 1, width))
@@ -370,23 +381,29 @@
     norm_out[...] = jnp.sum(norm_r[...], axis=0)
 
 
-def store_kernel(state, disp, sums, state_out, disp_out, norm_out, held, sem):
-    parts = 8
-    arrive = pltpu.make_async_copy(sums, held, sem.at[parts + 1])
-    arrive.start()
+def store_kernel(state, disp, sums, state_out, disp_out, norm_out, held, moved, added, get, put):
+    parts = get.shape[0] - 2
     rows = state.shape[0] // parts
-    copies = [pltpu.make_async_copy(disp, disp_out, sem.at[parts])]
+    blocks = [(sums, added, None), (disp, moved, disp_out)]
     for i in range(parts):
         part = pl.ds(i * rows, rows)
-        copies.append(pltpu.make_async_copy(state.at[part], state_out.at[part], sem.at[i]))
-    for copy in copies:
+        blocks.append((state.at[part], held.at[part], state_out.at[part]))
+    arrivals = [
+        pltpu.make_async_copy(here, kept, get.at[i]) for i, (here, kept, _) in enumerate(blocks)
+    ]
+    for copy in arrivals:
         copy.start()
-    arrive.wait()
-    roots = jnp.sqrt(held[...] + 1e-06)
+    leaves = []
+    for i, (_, kept, there) in enumerate(blocks):
+        arrivals[i].wait()
+        if there is not None:
+            leaves.append(pltpu.make_async_copy(kept, there, put.at[i]))
+            leaves[-1].start()
+    roots = jnp.sqrt(added[...] + 1e-06)
     across = iota(roots.shape, 1)
     for k in range(COUPLE):
         norm_out[k] = jnp.sum(jnp.where(across == k, roots, 0.0))
-    for copy in copies:
+    for copy in leaves:
         copy.wait()
 
 
@@ -470,7 +487,13 @@
             ),
             in_specs=[hbm] * 3,
             out_specs=(hbm, hbm, smem),
-            scratch_shapes=[pltpu.VMEM(sums.shape, f32), pltpu.SemaphoreType.DMA((10,))],
+            scratch_shapes=[
+                pltpu.VMEM(state.shape, f32),
+                pltpu.VMEM(disp.shape, f32),
+                pltpu.VMEM(sums.shape, f32),
+                pltpu.SemaphoreType.DMA((10,)),
+                pltpu.SemaphoreType.DMA((10,)),
+            ],
             compiler_params=pltpu.CompilerParams(vmem_limit_bytes=VMEM),
         )(state, disp, sums)
     )

time: 123 us -> 57.5 us (0.47)
  Pallas kernels: 122 us -> 56.7 us
    pallas_call x1, Pallas kernels: 67.2 us -> 2.99 us  [per_device(): pl.pallas_call(store_kernel, out_shape=(jax.ShapeDtypeStruct(state.shape,...]
    pallas_call x1, Pallas kernels: 55.2 us -> 53.7 us  [per_device(): pl.pallas_call(functools.partial(kernel, n, dom), out_shape=(jax.ShapeDty...]
where the time goes in v3:
time: 57.5 us; the launch traced here: 57.3 us
  Pallas kernels  56.7 us (99%)
  between operations  0.64 us (1%)
    pallas_call x1, Pallas kernels, per_device(): pl.pallas_call(functools.partial(kernel, n, dom), out_shape=(jax.ShapeDty...  53.7 us
    pallas_call x1, Pallas kernels, per_device(): pl.pallas_call(store_kernel, out_shape=(jax.ShapeDtypeStruct(state.shape,...  2.99 us

profile of v3, /device:TPU:0, one launch (start us, length us, event | category | flops | bytes accessed | tf_op | source)
XLA Modules:
  0.0 57.3 jit_solution(17693177607089342793)
XLA Ops:
  0.6 53.7 %shard_map.103 = (f32[128,32,128]{2,1,0:T(8,128)}, f32[128,128]{1,0:T(8,128)}, f32[1,128]{1,0:T(1,128)}) custom-call(f32[128,32,128]{2,1,0:T(8,128)} %source.1, s32[128,32,128]{2,1,0:T(8,128)} %ids.1, f32[16]{0:T(128)} %table_in.1, s32[1,128]{1,0:T(1,128)} %bitcast.2, s32[1,128]{1,0:T(1,128)} %bitcast.3, f32[128,128]{1,0:T(8,128)} %init_in.1, ...), custom_call_target="tpu_custom_call" | custom-call | tf_op jit(solution)/shard_map/pallas_call | solution.py:423
  54.3 3.0 %shard_map.104 = (f32[128,32,128]{2,1,0:T(8,128)}, f32[128,128]{1,0:T(8,128)}, f32[2]{0:T(128)}) custom-call(f32[128,32,128]{2,1,0:T(8,128)} %get-tuple-element.6.state, f32[128,128]{1,0:T(8,128)} %get-tuple-element.7.disp, f32[1,128]{1,0:T(1,128)} %get-tuple-element.8.sums), custom_call_target="tpu_custom_call" | custom-call | tf_op jit(solution)/shard_map/pallas_call | solution.py:481

commit v4 on v3

--- a/solution.py
+++ b/solution.py
@@ -81,14 +81,21 @@
     right = after(my_sect, my_dom)
     left = ahead(my_sect, my_dom)
 
+    def wrapped(value, count):
+        return jnp.where(value >= count, value - count, value)
+
+    dom_at = [wrapped(my_dom + step, dom) for step in range(dom)]
+
     def each_peer(act):
-        def one(k, at):
-            act(*at)
-            return after(*at)
-
-        beyond = jnp.where(my_sect + 1 == sect, 0, my_sect + 1)
-        at = lax.fori_loop(0, n - dom, one, (beyond, my_dom))
-        lax.fori_loop(1, dom, one, after(*at))
+        def one(step, carry):
+            sect_at = wrapped(my_sect + step, sect)
+            for at in dom_at:
+                act(sect_at, at)
+            return carry
+
+        lax.fori_loop(1, sect, one, 0)
+        for at in dom_at[1:]:
+            act(my_sect, at)
 
     loads = [
         pltpu.make_async_copy(a, b, in_sem.at[i])

time: 57.5 us -> 56.5 us (0.983)
  Pallas kernels: 56.7 us -> 55.7 us
    pallas_call x1, Pallas kernels: 53.7 us -> 52.7 us  [per_device(): pl.pallas_call(functools.partial(kernel, n, dom), out_shape=(jax.ShapeDty...]
where the time goes in v4:
time: 56.5 us; the launch traced here: 56.3 us
  Pallas kernels  55.7 us (99%)
  between operations  0.64 us (1%)
    pallas_call x1, Pallas kernels, per_device(): pl.pallas_call(functools.partial(kernel, n, dom), out_shape=(jax.ShapeDty...  52.7 us
    pallas_call x1, Pallas kernels, per_device(): pl.pallas_call(store_kernel, out_shape=(jax.ShapeDtypeStruct(state.shape,...  2.99 us

profile of v4, /device:TPU:0, one launch (start us, length us, event | category | flops | bytes accessed | tf_op | source)
XLA Modules:
  0.0 56.3 jit_solution(14594365009660044724)
XLA Ops:
  0.6 52.7 %shard_map.103 = (f32[128,32,128]{2,1,0:T(8,128)}, f32[128,128]{1,0:T(8,128)}, f32[1,128]{1,0:T(1,128)}) custom-call(f32[128,32,128]{2,1,0:T(8,128)} %source.1, s32[128,32,128]{2,1,0:T(8,128)} %ids.1, f32[16]{0:T(128)} %table_in.1, s32[1,128]{1,0:T(1,128)} %bitcast.2, s32[1,128]{1,0:T(1,128)} %bitcast.3, f32[128,128]{1,0:T(8,128)} %init_in.1, ...), custom_call_target="tpu_custom_call" | custom-call | tf_op jit(solution)/shard_map/pallas_call | solution.py:430
  53.3 3.0 %shard_map.104 = (f32[128,32,128]{2,1,0:T(8,128)}, f32[128,128]{1,0:T(8,128)}, f32[2]{0:T(128)}) custom-call(f32[128,32,128]{2,1,0:T(8,128)} %get-tuple-element.6.state, f32[128,128]{1,0:T(8,128)} %get-tuple-element.7.disp, f32[1,128]{1,0:T(1,128)} %get-tuple-element.8.sums), custom_call_target="tpu_custom_call" | custom-call | tf_op jit(solution)/shard_map/pallas_call | solution.py:488

commit v5 on v4

--- a/solution.py
+++ b/solution.py
@@ -13,6 +13,7 @@
 TOTAL = SWEEPS * COUPLE
 GHOST = TOTAL - 1
 PAD = 8
+STEP = 8
 VMEM = 58 * 2**20
 MESH = pl.DeviceIdType.MESH
 
@@ -148,11 +149,11 @@
         even[x] = src[x] * value
 
     def first_block(i, carry):
-        for j in range(4):
-            first(PAD + 4 * i + j, None)
+        for j in range(STEP):
+            first(PAD + STEP * i + j, None)
         return carry
 
-    lax.fori_loop(0, rows // 4, first_block, 0)
+    lax.fori_loop(0, rows // STEP, first_block, 0)
     pl.semaphore_wait(barrier, n - 1)
 
     def exchange(sent, got, phase):
@@ -198,29 +199,35 @@
             lambda i: ghost_ss.at[number, i], lambda i: ghost_rs.at[number, i],
         )
 
-    row = iota((depth, width), 0)
+    low_row = iota((8, width), 0) == 0
+    high_row = iota((8, width), 0) == 7
 
     def sweep(number, begin, stop):
         old, new = (even, odd) if number % 2 == 1 else (odd, even)
         count = stop - begin
+
+        flat = old.reshape(old.shape[0] * depth, width)
 
         def planes(x, many):
             held = [old[x - 1 + j] for j in range(many + 2)]
             for j in range(many):
                 here = held[j + 1]
+                at = (x + j) * depth
+                up = flat[pl.ds(at - 1, depth), :]
+                down = flat[pl.ds(at + 1, depth), :]
+                up = jnp.concatenate([jnp.where(low_row, 0.0, up[:8]), up[8:]], axis=0)
+                down = jnp.concatenate([down[:-8], jnp.where(high_row, 0.0, down[-8:])], axis=0)
                 total = src[x + j] + (held[j] + held[j + 2])
-                up = jnp.where(row == 0, 0.0, pltpu.roll(here, 1, 0))
-                down = jnp.where(row == depth - 1, 0.0, pltpu.roll(here, depth - 1, 0))
                 total = total + (up + down) + beside(here)
                 new[x + j] = total * inv[x + j]
 
         def block(i, carry):
-            planes(begin + 4 * i, 4)
+            planes(begin + STEP * i, STEP)
             return carry
 
-        lax.fori_loop(0, count // 4, block, 0)
-        if count % 4:
-            planes(begin + count // 4 * 4, count % 4)
+        lax.fori_loop(0, count // STEP, block, 0)
+        if count % STEP:
+            planes(begin + count // STEP * STEP, count % STEP)
 
     def whole(number):
         sweep(number, PAD - (GHOST - number), end + (GHOST - number))

time: 56.5 us -> 52.6 us (0.931)
  Pallas kernels: 55.7 us -> 51.8 us
    pallas_call x1, Pallas kernels: 52.7 us -> 48.8 us  [per_device(): pl.pallas_call(functools.partial(kernel, n, dom), out_shape=(jax.ShapeDty...]
where the time goes in v5:
time: 52.6 us; the launch traced here: 52.5 us
  Pallas kernels  51.8 us (98%)
  between operations  0.64 us (1%)
    pallas_call x1, Pallas kernels, per_device(): pl.pallas_call(functools.partial(kernel, n, dom), out_shape=(jax.ShapeDty...  48.8 us
    pallas_call x1, Pallas kernels, per_device(): pl.pallas_call(store_kernel, out_shape=(jax.ShapeDtypeStruct(state.shape,...  2.99 us

profile of v5, /device:TPU:0, one launch (start us, length us, event | category | flops | bytes accessed | tf_op | source)
XLA Modules:
  0.0 52.5 jit_solution(8200586281085678243)
XLA Ops:
  0.6 48.8 %shard_map.103 = (f32[128,32,128]{2,1,0:T(8,128)}, f32[128,128]{1,0:T(8,128)}, f32[1,128]{1,0:T(1,128)}) custom-call(f32[128,32,128]{2,1,0:T(8,128)} %source.1, s32[128,32,128]{2,1,0:T(8,128)} %ids.1, f32[16]{0:T(128)} %table_in.1, s32[1,128]{1,0:T(1,128)} %bitcast.2, s32[1,128]{1,0:T(1,128)} %bitcast.3, f32[128,128]{1,0:T(8,128)} %init_in.1, ...), custom_call_target="tpu_custom_call" | custom-call | tf_op jit(solution)/shard_map/pallas_call | solution.py:437
  49.5 3.0 %shard_map.104 = (f32[128,32,128]{2,1,0:T(8,128)}, f32[128,128]{1,0:T(8,128)}, f32[2]{0:T(128)}) custom-call(f32[128,32,128]{2,1,0:T(8,128)} %get-tuple-element.6.state, f32[128,128]{1,0:T(8,128)} %get-tuple-element.7.disp, f32[1,128]{1,0:T(1,128)} %get-tuple-element.8.sums), custom_call_target="tpu_custom_call" | custom-call | tf_op jit(solution)/shard_map/pallas_call | solution.py:495

commit v6 on v5

--- a/solution.py
+++ b/solution.py
@@ -13,7 +13,7 @@
 TOTAL = SWEEPS * COUPLE
 GHOST = TOTAL - 1
 PAD = 8
-STEP = 8
+STEP = 16
 VMEM = 58 * 2**20
 MESH = pl.DeviceIdType.MESH
 
@@ -149,11 +149,11 @@
         even[x] = src[x] * value
 
     def first_block(i, carry):
-        for j in range(STEP):
-            first(PAD + STEP * i + j, None)
+        for j in range(PAD):
+            first(PAD + PAD * i + j, None)
         return carry
 
-    lax.fori_loop(0, rows // STEP, first_block, 0)
+    lax.fori_loop(0, rows // PAD, first_block, 0)
     pl.semaphore_wait(barrier, n - 1)
 
     def exchange(sent, got, phase):
@@ -199,6 +199,14 @@
             lambda i: ghost_ss.at[number, i], lambda i: ghost_rs.at[number, i],
         )
 
+    def column(ref, begin, count, y):
+        flat = ref.reshape(ref.shape[0] * depth, width)
+        return flat, pl.ds(begin * depth + y, count, stride=depth)
+
+    def take(ref, begin, count, y):
+        flat, where = column(ref, begin, count, y)
+        return flat[where, :]
+
     low_row = iota((8, width), 0) == 0
     high_row = iota((8, width), 0) == 7
 
@@ -221,20 +229,24 @@
                 total = total + (up + down) + beside(here)
                 new[x + j] = total * inv[x + j]
 
+        blocks = -(-count // STEP)
+        step = -(-count // blocks)
+
         def block(i, carry):
-            planes(begin + STEP * i, STEP)
+            planes(jnp.where(i == blocks - 1, stop - step, begin + step * i), step)
             return carry
 
-        lax.fori_loop(0, count // STEP, block, 0)
-        if count % STEP:
-            planes(begin + count // STEP * STEP, count % STEP)
+        if blocks == 1:
+            planes(begin, count)
+        else:
+            lax.fori_loop(0, blocks, block, 0)
 
     def whole(number):
         sweep(number, PAD - (GHOST - number), end + (GHOST - number))
 
     def tractions(number):
         new = odd if number % 2 == 1 else even
-        base[number // SWEEPS] = new[PAD:end, 0, :] - new[PAD:end, 1, :]
+        base[number // SWEEPS] = take(new, PAD, rows, 0) - take(new, PAD, rows, 1)
 
     for x in list(range(PAD - GHOST)) + list(range(end + GHOST, end + PAD)):
         inv[x] = jnp.zeros((depth, width), jnp.float32)
@@ -258,7 +270,7 @@
         first(PAD - GHOST + x, low_scale)
         first(end + x, high_scale)
     for y in range(TOTAL):
-        invp[y] = inv[:, y, :]
+        invp[y] = take(inv, 0, rows + 2 * PAD, y)
 
     def wall_of(k):
         finish(wall_r.at[k], a2a_rs.at[1 + 2 * k])
@@ -364,7 +376,8 @@
     bulk.start()
     planes, edges2 = iterate(1, [force[y] for y in range(SWEEPS)])
     for y in range(TOTAL):
-        last[PAD:end, y, :] = last[PAD:end, y, :] + planes[y][PAD:end, :]
+        flat, where = column(last, PAD, rows, y)
+        flat[where, :] = flat[where, :] + planes[y][PAD:end, :]
     top = pltpu.make_async_copy(
         last.at[pl.ds(PAD, rows), pl.ds(0, PAD)],
         state_out.at[:, pl.ds(0, PAD)],

time: 52.6 us -> 52.4 us (level)
  no operation moved by 1% of the time
where the time goes in v6:
time: 52.4 us; the launch traced here: 52.2 us
  Pallas kernels  51.6 us (98%)
  between operations  0.64 us (1%)
    pallas_call x1, Pallas kernels, per_device(): pl.pallas_call(functools.partial(kernel, n, dom), out_shape=(jax.ShapeDty...  48.6 us
    pallas_call x1, Pallas kernels, per_device(): pl.pallas_call(store_kernel, out_shape=(jax.ShapeDtypeStruct(state.shape,...  2.99 us

profile of v6, /device:TPU:0, one launch (start us, length us, event | category | flops | bytes accessed | tf_op | source)
XLA Modules:
  0.0 52.2 jit_solution(13056277100504339920)
XLA Ops:
  0.6 48.6 %shard_map.103 = (f32[128,32,128]{2,1,0:T(8,128)}, f32[128,128]{1,0:T(8,128)}, f32[1,128]{1,0:T(1,128)}) custom-call(f32[128,32,128]{2,1,0:T(8,128)} %source.1, s32[128,32,128]{2,1,0:T(8,128)} %ids.1, f32[16]{0:T(128)} %table_in.1, s32[1,128]{1,0:T(1,128)} %bitcast.2, s32[1,128]{1,0:T(1,128)} %bitcast.3, f32[128,128]{1,0:T(8,128)} %init_in.1, ...), custom_call_target="tpu_custom_call" | custom-call | tf_op jit(solution)/shard_map/pallas_call | solution.py:450
  49.2 3.0 %shard_map.104 = (f32[128,32,128]{2,1,0:T(8,128)}, f32[128,128]{1,0:T(8,128)}, f32[2]{0:T(128)}) custom-call(f32[128,32,128]{2,1,0:T(8,128)} %get-tuple-element.6.state, f32[128,128]{1,0:T(8,128)} %get-tuple-element.7.disp, f32[1,128]{1,0:T(1,128)} %get-tuple-element.8.sums), custom_call_target="tpu_custom_call" | custom-call | tf_op jit(solution)/shard_map/pallas_call | solution.py:508

commit v7 on v6

--- a/solution.py
+++ b/solution.py
@@ -308,12 +308,13 @@
 
         return plane
 
-    def iterate(k, begun):
+    def iterate(k, begun, meanwhile):
         mine, edges = wall_of(k)
         margin = jnp.zeros((PAD, width), jnp.float32)
         own = spread(jnp.concatenate([margin, mine, margin], axis=0), begun, lambda y: invp[y])
-        traction = base[k] + (own(SWEEPS, 0) - own(SWEEPS, 1))[PAD:end, :]
-        trac[...] = traction
+        trac[...] = (own(SWEEPS, 0) - own(SWEEPS, 1))[PAD:end, :]
+        meanwhile()
+        trac[...] = trac[...] + base[k]
         for copy in edges:
             copy.wait_recv()
 
@@ -352,29 +353,38 @@
 
     sweep(1, PAD - GHOST + 1, PAD + 1)
     sweep(1, end - 1, end + GHOST - 1)
-    whole(2)
-    tractions(2)
-    planes, edges = iterate(0, [])
+    half = PAD + rows // 2
+    sweep(2, PAD - GHOST + 2, half)
+
+    def rest_of_2():
+        sweep(2, half, end + GHOST - 2)
+        tractions(2)
+
+    planes, edges = iterate(0, [], rest_of_2)
     for y in range(SWEEPS):
         force[y] = planes[y]
     whole(3)
-    sweep(4, PAD - 1, PAD + rows // 2)
+    sweep(4, PAD - 1, half)
     displacement, mismatch = solid(0, init[...])
     wall_s[1] = pick(choose[...], displacement).reshape(n, cap, width)
     exchange(wall_s.at[1], wall_r.at[1], 3)
     disp[...] = displacement
     part0 = squares(mismatch)
-    sweep(4, PAD + rows // 2, end + 1)
-    whole(5)
-    tractions(5)
+    sweep(4, half, end + 1)
+    sweep(5, PAD, half)
     last = odd if GHOST % 2 == 1 else even
     bulk = pltpu.make_async_copy(
         last.at[pl.ds(PAD, rows), pl.ds(PAD, depth - PAD)],
         state_out.at[:, pl.ds(PAD, depth - PAD)],
         out_sem.at[0],
     )
-    bulk.start()
-    planes, edges2 = iterate(1, [force[y] for y in range(SWEEPS)])
+
+    def rest_of_5():
+        sweep(5, half, end)
+        tractions(5)
+        bulk.start()
+
+    planes, edges2 = iterate(1, [force[y] for y in range(SWEEPS)], rest_of_5)
     for y in range(TOTAL):
         flat, where = column(last, PAD, rows, y)
         flat[where, :] = flat[where, :] + planes[y][PAD:end, :]

time: 52.4 us -> 52.3 us (level)
  no operation moved by 1% of the time
where the time goes in v7:
time: 52.3 us; the launch traced here: 52.2 us
  Pallas kernels  51.5 us (98%)
  between operations  0.64 us (1%)
    pallas_call x1, Pallas kernels, per_device(): pl.pallas_call(functools.partial(kernel, n, dom), out_shape=(jax.ShapeDty...  48.5 us
    pallas_call x1, Pallas kernels, per_device(): pl.pallas_call(store_kernel, out_shape=(jax.ShapeDtypeStruct(state.shape,...  2.99 us

profile of v7, /device:TPU:0, one launch (start us, length us, event | category | flops | bytes accessed | tf_op | source)
XLA Modules:
  0.0 52.2 jit_solution(8831463628419222257)
XLA Ops:
  0.6 48.5 %shard_map.103 = (f32[128,32,128]{2,1,0:T(8,128)}, f32[128,128]{1,0:T(8,128)}, f32[1,128]{1,0:T(1,128)}) custom-call(f32[128,32,128]{2,1,0:T(8,128)} %source.1, s32[128,32,128]{2,1,0:T(8,128)} %ids.1, f32[16]{0:T(128)} %table_in.1, s32[1,128]{1,0:T(1,128)} %bitcast.2, s32[1,128]{1,0:T(1,128)} %bitcast.3, f32[128,128]{1,0:T(8,128)} %init_in.1, ...), custom_call_target="tpu_custom_call" | custom-call | tf_op jit(solution)/shard_map/pallas_call | solution.py:460
  49.2 3.0 %shard_map.104 = (f32[128,32,128]{2,1,0:T(8,128)}, f32[128,128]{1,0:T(8,128)}, f32[2]{0:T(128)}) custom-call(f32[128,32,128]{2,1,0:T(8,128)} %get-tuple-element.6.state, f32[128,128]{1,0:T(8,128)} %get-tuple-element.7.disp, f32[1,128]{1,0:T(1,128)} %get-tuple-element.8.sums), custom_call_target="tpu_custom_call" | custom-call | tf_op jit(solution)/shard_map/pallas_call | solution.py:518
